TPU v7x, 32 devices: a whole 2x2x4 slice. The times are simulated.
32 devices in a mesh: section: 2 (over core), dp: 16 (over z, y, x).
Axes of the slice: x: 2, y: 2, z: 4, core: 2. Of those that a mesh axis runs over, the one named last changes fastest.
Arguments:
- canvases: bfloat16 [2, 128, 96, 2048], P('section', 'dp')
- crop_starts: int32 [2, 4], replicated, may hold values from 0 to 95, as said below
- pixel_mask: int32 [2, 128, 96], P(None, 'dp'), may hold values from 0 to 1, as said below
- drop_bits: int32 [2, 128, 96, 2048], P(None, 'dp'), may hold values from 0 to 1023
- reduce_weight: bfloat16 [2, 2048, 512], P('section'), may hold values from -0.125 to 0.125
- spatial_weight: bfloat16 [2, 9, 512, 512], P('section'), may hold values from -0.09375 to 0.09375
- expand_weight: bfloat16 [2, 512, 2048], P('section'), may hold values from -0.25 to 0.25
- inner_gain: float32 [2, 2, 512], P('section'), may hold values from 0.25 to 1.75
- inner_bias: float32 [2, 2, 512], P('section'), may hold values from -3 to 3
- outer_gain: float32 [2, 2048], P('section'), may hold values from 0.25 to 1.75
- outer_bias: float32 [2, 2048], P('section'), may hold values from -3 to 3
- head_weight: bfloat16 [2048, 48], replicated, may hold values from -0.3984375 to 0.3984375
- head_bias: float32 [48], replicated, may hold values from -4 to 4
- head_cotangent: bfloat16 [2, 128, 96, 48], P(None, 'dp'), may hold values from -5 to 5
Outputs:
- heads: float32 [2, 128, 96, 48], P('section', 'dp')
- canvas_grad: bfloat16 [2, 128, 96, 2048], P('section', 'dp')
- reduce_grad: float32 [2, 2048, 512], P('section')
- spatial_grad: float32 [2, 9, 512, 512], P('section')
- expand_grad: float32 [2, 512, 2048], P('section')
- inner_gain_grad: float32 [2, 2, 512], P('section')
- inner_bias_grad: float32 [2, 2, 512], P('section')
- outer_gain_grad: float32 [2, 2048], P('section')
- outer_bias_grad: float32 [2, 2048], P('section')
- head_weight_grad: float32 [2048, 48], P('section')
- head_bias_grad: float32 [48], P('section')
Inputs may be any that keep to these rules, and one draw needn't show every extreme that they name: crop_starts[b, 0] is 0 and each row strictly increases; crop k of canvas b spans all 128 rows and the columns from its start up to the next start, or up to 96. `pixel_mask`: column 0 of every canvas row is live.
All inputs are finite; a program needn't handle non-finite values.
Results may differ from a plain program's by a relative error of at most 0.015.
Values may be sent and summed in bfloat16 or wider, within the bound.
A program may use at most 320 MiB of HBM per device.

v0:
```python
import jax
import jax.numpy as jnp
from jax import lax
from jax.sharding import PartitionSpec as P

TASKS = 3
HEAD_OUT = 16
MB = 2


EPS = 1e-05
SOFT = 0.05
SHARP = 0.1
LEVELS = 1024.0
ACROSS = (((0,), (0,)), ((), ()))
BESIDE = (((1,), (1,)), ((), ()))


def extended(x, sides, width):
    for axis, dim in sides:
        size, length = (lax.axis_size(axis), x.shape[dim])
        up = [(i, (i + 1) % size) for i in range(size - 1)]
        down = [(j, i) for i, j in up]
        last = lax.slice_in_dim(x, length - width, length, axis=dim)
        leading = lax.slice_in_dim(x, 0, width, axis=dim)
        before = lax.ppermute(last, axis, up)
        after = lax.ppermute(leading, axis, down)
        x = jnp.concatenate([before, x, after], axis=dim)
    return x


def passed_along(block, axis, distance):
    devices = range(lax.axis_size(axis))
    route = [(i - distance, i) for i in devices if i - distance in devices]
    return lax.ppermute(block, axis, route)


def silu_slope(values):
    sigma = jax.nn.sigmoid(values)
    return sigma * (1.0 + values * (1.0 - sigma))


def column_masks(starts, width):
    columns = jnp.arange(width, dtype=jnp.int32)
    crop = jnp.sum((columns[:, None] >= starts[None, :]).astype(jnp.int32), axis=1)
    outside = jnp.full((1,), -1, jnp.int32)
    before = jnp.concatenate([outside, crop[:-1]])
    after = jnp.concatenate([crop[1:], outside])
    return [
        (before == crop).astype(jnp.bfloat16),
        jnp.ones((width,), jnp.bfloat16),
        (after == crop).astype(jnp.bfloat16),
    ]


def patches(padded, masks, sign):
    rows = padded.shape[0] - 2
    width = padded.shape[1]
    wide = jnp.pad(padded, ((0, 0), (1, 1), (0, 0)))
    blocks = []
    for row_step in range(3):
        for col_step in range(3):
            top = 1 + sign * (row_step - 1)
            left = 1 + sign * (col_step - 1)
            piece = wide[top : top + rows, left : left + width]
            if col_step != 1:
                piece = piece * masks[1 + sign * (col_step - 1)][None, :, None]
            blocks.append(piece)
    return jnp.concatenate(blocks, axis=2).reshape(rows * width, -1)


def pick(array, index):
    return lax.dynamic_index_in_dim(array, index, 0, keepdims=False)


def norm_forward(values, weights, local_count):
    total, count = lax.psum((jnp.sum(values * weights, axis=0), local_count), "dp")
    mean = total / count
    centered = values - mean
    spread = lax.psum(jnp.sum(weights * centered * centered, axis=0), "dp") / count
    scale = lax.rsqrt(spread + EPS)
    return (centered * scale, scale, count)


def norm_backward(upstream, normed, weights, count, gain, scale):
    bias_sum, gain_sum = lax.psum(
        (jnp.sum(upstream, axis=0), jnp.sum(upstream * normed, axis=0)), "dp"
    )
    result = scale * gain * (upstream - weights * (bias_sum + normed * gain_sum) / count)
    return (result, gain_sum, bias_sum)


def graddrop(task_grads, bits):
    soft = [jnp.sqrt(value * value + SOFT * SOFT) for value in task_grads]
    signed = task_grads[0]
    magnitude = soft[0]
    for index in range(1, len(task_grads)):
        signed = signed + task_grads[index]
        magnitude = magnitude + soft[index]
    purity = 0.5 * (1.0 + signed / magnitude)
    level = (bits.astype(jnp.float32) + 0.5) / LEVELS
    keep = jax.nn.sigmoid((purity - level) / SHARP)
    merged = jnp.zeros_like(purity)
    for value, scale in zip(task_grads, soft):
        upward = 0.5 * (1.0 + value / scale)
        merged = merged + value * (keep * upward + (1.0 - keep) * (1.0 - upward))
    return merged


def layer_forward(layer_in, params, weights, masks):
    (
        reduce_kernel,
        spatial_flat,
        spatial_back,
        expand_kernel,
        gain_in,
        bias_in,
        gain_out,
        bias_out,
    ) = params
    rows, width, channels = layer_in.shape
    flat_in = layer_in.reshape(rows * width, channels)
    local_count = jnp.sum(weights)
    first_map = jnp.dot(flat_in, reduce_kernel, preferred_element_type=jnp.float32)
    normed_a, scale_a, count = norm_forward(first_map, weights, local_count)
    act_a = jax.nn.silu(gain_in[0] * normed_a + bias_in[0]).astype(jnp.bfloat16)
    padded = extended(act_a.reshape(rows, width, -1), (("dp", 0),), 1)
    second_map = jnp.dot(
        patches(padded, masks, 1), spatial_flat, preferred_element_type=jnp.float32
    )
    normed_b, scale_b, count = norm_forward(second_map, weights, local_count)
    act_b = jax.nn.silu(gain_in[1] * normed_b + bias_in[1]).astype(jnp.bfloat16)
    third_map = jnp.dot(act_b, expand_kernel, preferred_element_type=jnp.float32)
    normed_c, scale_c, count = norm_forward(third_map, weights, local_count)
    output = jax.nn.silu(gain_out * normed_c + bias_out + flat_in.astype(jnp.float32))
    return (
        output,
        (flat_in, normed_a, scale_a, padded, normed_b, scale_b, normed_c, scale_c, count),
    )


def layer_backward(grad_out, kept, params, weights, masks):
    (
        reduce_kernel,
        spatial_flat,
        spatial_back,
        expand_kernel,
        gain_in,
        bias_in,
        gain_out,
        bias_out,
    ) = params
    flat_in, normed_a, scale_a, padded, normed_b, scale_b, normed_c, scale_c, count = kept
    rows, width = (padded.shape[0] - 2, padded.shape[1])
    grad_t = grad_out * silu_slope(gain_out * normed_c + bias_out + flat_in.astype(jnp.float32))
    grad_c, gain_c, bias_c = norm_backward(grad_t, normed_c, weights, count, gain_out, scale_c)
    grad_c = grad_c.astype(jnp.bfloat16)
    affine_b = gain_in[1] * normed_b + bias_in[1]
    act_b = jax.nn.silu(affine_b).astype(jnp.bfloat16)
    expand_part = lax.dot_general(act_b, grad_c, ACROSS, preferred_element_type=jnp.float32)
    grad_act_b = lax.dot_general(grad_c, expand_kernel, BESIDE, preferred_element_type=jnp.float32)
    grad_b, gain_b, bias_b = norm_backward(
        grad_act_b * silu_slope(affine_b), normed_b, weights, count, gain_in[1], scale_b
    )
    grad_b = grad_b.astype(jnp.bfloat16)
    spatial_part = lax.dot_general(
        patches(padded, masks, 1), grad_b, ACROSS, preferred_element_type=jnp.float32
    )
    grad_pad = extended(grad_b.reshape(rows, width, -1), (("dp", 0),), 1)
    grad_act_a = jnp.dot(
        patches(grad_pad, masks, -1), spatial_back, preferred_element_type=jnp.float32
    )
    affine_a = gain_in[0] * normed_a + bias_in[0]
    grad_a, gain_a, bias_a = norm_backward(
        grad_act_a * silu_slope(affine_a), normed_a, weights, count, gain_in[0], scale_a
    )
    grad_a = grad_a.astype(jnp.bfloat16)
    reduce_part = lax.dot_general(flat_in, grad_a, ACROSS, preferred_element_type=jnp.float32)
    grad_in = (
        lax.dot_general(grad_a, reduce_kernel, BESIDE, preferred_element_type=jnp.float32) + grad_t
    )
    return (
        grad_in.astype(jnp.bfloat16),
        (reduce_part, spatial_part, expand_part),
        (gain_a, gain_b, bias_a, bias_b, gain_c, bias_c),
    )


def heads_step(feature, head_weight, head_bias, cotangent, weights, bits):
    heads = jnp.dot(feature, head_weight, preferred_element_type=jnp.float32) + head_bias
    target = cotangent * weights.astype(jnp.bfloat16)
    weight_part = lax.dot_general(feature, target, ACROSS, preferred_element_type=jnp.float32)
    bias_part = jnp.sum(target.astype(jnp.float32), axis=0)
    task_grads = []
    for task in range(TASKS):
        start = task * HEAD_OUT
        task_grads.append(
            lax.dot_general(
                target[:, start : start + HEAD_OUT],
                head_weight[:, start : start + HEAD_OUT],
                BESIDE,
                preferred_element_type=jnp.float32,
            )
        )
    return (heads, graddrop(task_grads, bits), weight_part, bias_part)


def local(
    canvases,
    crop_starts,
    pixel_mask,
    drop_bits,
    reduce_weight,
    spatial_weight,
    expand_weight,
    inner_gain,
    inner_bias,
    outer_gain,
    outer_bias,
    head_weight,
    head_bias,
    head_cotangent,
):
    section = lax.axis_index("section")
    first = section == 0
    half = canvases.shape[0]
    rows, width, channels = (canvases.shape[1], canvases.shape[2], canvases.shape[3])
    inner = reduce_weight.shape[2]
    pixels = rows * width
    head_cols = head_weight.shape[1]
    kernel = spatial_weight[0]
    params = (
        reduce_weight[0],
        kernel.reshape(9 * inner, inner),
        jnp.swapaxes(kernel, 1, 2).reshape(9 * inner, inner),
        expand_weight[0],
        inner_gain[0],
        inner_bias[0],
        outer_gain[0],
        outer_bias[0],
    )
    arriving = passed_along(canvases, "section", -1)
    inputs = jnp.concatenate([canvases, arriving], axis=0)
    silent = jnp.zeros((rows, width, channels), jnp.bfloat16)
    received = silent
    head_w_sum = jnp.zeros((channels, head_cols), jnp.float32)
    head_b_sum = jnp.zeros((head_cols,), jnp.float32)
    saved = []
    for tick in range(MB + 1):
        batch = tick - section
        valid = jnp.logical_and(batch >= 0, batch < MB).astype(jnp.float32)
        index = jnp.clip(batch, 0, MB - 1)
        weights = pick(pixel_mask, index).reshape(pixels, 1).astype(jnp.float32)
        masks = column_masks(pick(crop_starts, index), width)
        own = inputs[tick] if tick < MB else silent
        layer_in = jnp.where(first, own, received)
        output, kept = layer_forward(layer_in, params, weights, masks)
        feature = output.astype(jnp.bfloat16)
        if tick < MB:
            received = passed_along(feature.reshape(rows, width, channels), "section", 1)
        cotangent = pick(head_cotangent, index).reshape(pixels, head_cols)
        bits = pick(drop_bits, index).reshape(pixels, channels)
        heads, merged, weight_part, bias_part = heads_step(
            feature, head_weight, head_bias, cotangent, weights, bits
        )
        head_w_sum = head_w_sum + valid * weight_part
        head_b_sum = head_b_sum + valid * bias_part
        saved.append((kept, merged, heads, weights, masks, valid))
    reduce_sum = jnp.zeros((channels, inner), jnp.float32)
    spatial_sum = jnp.zeros((9 * inner, inner), jnp.float32)
    expand_sum = jnp.zeros((inner, channels), jnp.float32)
    norm_sums = [jnp.zeros((inner,), jnp.float32)] * 4 + [jnp.zeros((channels,), jnp.float32)] * 2
    back = silent
    returned = [None] * MB
    for step in range(MB + 1):
        tick = MB - step
        kept, merged, heads, weights, masks, valid = saved[tick]
        grad_out = jnp.where(first, back.reshape(pixels, channels).astype(jnp.float32), merged)
        grad_in, kernel_parts, norm_parts = layer_backward(grad_out, kept, params, weights, masks)
        grad_in = grad_in.reshape(rows, width, channels)
        if step < MB:
            back = passed_along(grad_in, "section", -1)
        if step >= 1:
            returned[MB - step] = grad_in
        norm_sums = [total + valid * part for total, part in zip(norm_sums, norm_parts)]
        reduce_sum = reduce_sum + valid * kernel_parts[0]
        spatial_sum = spatial_sum + valid * kernel_parts[1]
        expand_sum = expand_sum + valid * kernel_parts[2]
    reduce_total, spatial_total, expand_total, head_w_total, head_b_total = lax.psum(
        (reduce_sum, spatial_sum, expand_sum, head_w_sum, head_b_sum), "dp"
    )
    own_grad = jnp.stack(returned[:half])
    later_grad = jnp.stack(returned[half:])
    arriving_grad = passed_along(later_grad, "section", 1)
    canvas_grad = jnp.where(first, own_grad, arriving_grad)
    front_heads = jnp.stack([saved[1][2]]).reshape(half, rows, width, head_cols)
    later_heads = jnp.stack([saved[2][2]]).reshape(half, rows, width, head_cols)
    split_rows = channels // 2
    split_cols = head_cols // 2
    came_heads, came_weight, came_bias = (
        passed_along(front_heads.astype(jnp.bfloat16), "section", -1).astype(front_heads.dtype),
        passed_along(head_w_total[:split_rows].astype(jnp.bfloat16), "section", -1).astype(
            jnp.float32
        ),
        passed_along(head_b_total[:split_cols].astype(jnp.bfloat16), "section", -1).astype(
            jnp.float32
        ),
    )
    heads_out = jnp.where(first, came_heads, later_heads)
    head_w_out = jnp.where(first, came_weight, head_w_total[split_rows:])
    head_b_out = jnp.where(first, came_bias, head_b_total[split_cols:])
    gain_a, gain_b, bias_a, bias_b, gain_c, bias_c = norm_sums
    return (
        heads_out,
        canvas_grad,
        reduce_total[None],
        spatial_total.reshape(9, inner, inner)[None],
        expand_total[None],
        jnp.stack([gain_a, gain_b])[None],
        jnp.stack([bias_a, bias_b])[None],
        gain_c[None],
        bias_c[None],
        head_w_out,
        head_b_out,
    )


def solution(mesh):
    placed = (
        P("section", "dp", None, None),
        P(),
        P(None, "dp", None),
        P(None, "dp", None, None),
        P("section", None, None),
        P("section", None, None, None),
        P("section", None, None),
        P("section", None, None),
        P("section", None, None),
        P("section", None),
        P("section", None),
        P(),
        P(),
        P(None, "dp", None, None),
    )
    return jax.shard_map(
        local,
        mesh=mesh,
        in_specs=placed,
        out_specs=(
            P("section", "dp", None, None),
            P("section", "dp", None, None),
            P("section", None, None),
            P("section", None, None, None),
            P("section", None, None),
            P("section", None, None),
            P("section", None, None),
            P("section", None),
            P("section", None),
            P("section", None),
            P("section"),
        ),
        check_vma=False,
    )
```

profile of v0, /device:TPU:0, one launch (start us, length us, event | category | flops | bytes accessed | tf_op | source)
XLA Modules:
  0.0 2117.9 jit_solution(13705959059484101542)
XLA Ops:
  19.4 44.1 %all-reduce.17 = (f32[512]{0:T(512)S(1)}, f32[]{:T(128)}) all-reduce(f32[512]{0:T(512)S(1)} %get-tuple-element.198, f32[]{:T(128)} %reduce_sum.406), channel_id=1, replica_groups=mesh['section'=2,'dp'=16] {'dp'}, use_global_device_ids=true, to_apply=%region_1.2 | all-reduce | flops 513 | bytes 4104 | tf_op jit(solution)/shard_map/psum | solution.py:77
  125.1 37.5 %psum.329 = f32[512]{0:T(512)S(1)} all-reduce(f32[512]{0:T(512)S(1)} %get-tuple-element.200), channel_id=1, replica_groups=mesh['section'=2,'dp'=16] {'dp'}, use_global_device_ids=true, to_apply=%region_8.9 | all-reduce | flops 512 | bytes 4096 | tf_op jit(solution)/shard_map/psum | solution.py:77
  165.0 37.6 %psum.330 = f32[512]{0:T(512)S(1)} all-reduce(f32[512]{0:T(512)S(1)} %fusion.51), channel_id=1, replica_groups=mesh['section'=2,'dp'=16] {'dp'}, use_global_device_ids=true, to_apply=%region_10.11 | all-reduce | flops 512 | bytes 4096 | tf_op jit(solution)/shard_map/psum | solution.py:80
  210.0 38.1 %psum.331 = f32[2048]{0:T(1024)S(1)} all-reduce(f32[2048]{0:T(1024)S(1)} %get-tuple-element.202), channel_id=1, replica_groups=mesh['section'=2,'dp'=16] {'dp'}, use_global_device_ids=true, to_apply=%region_12.13 | all-reduce | flops 2048 | bytes 16384 | tf_op jit(solution)/shard_map/psum | solution.py:77
  252.5 38.1 %psum.332 = f32[2048]{0:T(1024)S(1)} all-reduce(f32[2048]{0:T(1024)S(1)} %fusion), channel_id=1, replica_groups=mesh['section'=2,'dp'=16] {'dp'}, use_global_device_ids=true, to_apply=%region_14.15 | all-reduce | flops 2048 | bytes 16384 | tf_op jit(solution)/shard_map/psum | solution.py:80
  310.0 38.2 %all-reduce.16 = (f32[512]{0:T(512)S(1)}, f32[]{:T(128)}) all-reduce(f32[512]{0:T(512)S(1)} %get-tuple-element.204, f32[]{:T(128)} %reduce_sum.414), channel_id=1, replica_groups=mesh['section'=2,'dp'=16] {'dp'}, use_global_device_ids=true, to_apply=%region_16.17 | all-reduce | flops 513 | bytes 4104 | tf_op jit(solution)/shard_map/psum | solution.py:77
  350.7 37.6 %psum.335 = f32[512]{0:T(512)S(1)} all-reduce(f32[512]{0:T(512)S(1)} %fusion.52), channel_id=1, replica_groups=mesh['section'=2,'dp'=16] {'dp'}, use_global_device_ids=true, to_apply=%region_20.21 | all-reduce | flops 512 | bytes 4096 | tf_op jit(solution)/shard_map/psum | solution.py:80
  409.9 37.6 %psum.336 = f32[512]{0:T(512)S(1)} all-reduce(f32[512]{0:T(512)S(1)} %get-tuple-element.206), channel_id=1, replica_groups=mesh['section'=2,'dp'=16] {'dp'}, use_global_device_ids=true, to_apply=%region_23.24 | all-reduce | flops 512 | bytes 4096 | tf_op jit(solution)/shard_map/psum | solution.py:77
  449.9 37.5 %psum.337 = f32[512]{0:T(512)S(1)} all-reduce(f32[512]{0:T(512)S(1)} %fusion.53), channel_id=1, replica_groups=mesh['section'=2,'dp'=16] {'dp'}, use_global_device_ids=true, to_apply=%region_25.26 | all-reduce | flops 512 | bytes 4096 | tf_op jit(solution)/shard_map/psum | solution.py:80
  494.7 38.2 %psum.338 = f32[2048]{0:T(1024)S(1)} all-reduce(f32[2048]{0:T(1024)S(1)} %get-tuple-element.208), channel_id=1, replica_groups=mesh['section'=2,'dp'=16] {'dp'}, use_global_device_ids=true, to_apply=%region_27.28 | all-reduce | flops 2048 | bytes 16384 | tf_op jit(solution)/shard_map/psum | solution.py:77
  537.3 38.1 %psum.339 = f32[2048]{0:T(1024)S(1)} all-reduce(f32[2048]{0:T(1024)S(1)} %fusion.1), channel_id=1, replica_groups=mesh['section'=2,'dp'=16] {'dp'}, use_global_device_ids=true, to_apply=%region_29.30 | all-reduce | flops 2048 | bytes 16384 | tf_op jit(solution)/shard_map/psum | solution.py:80
  618.0 38.2 %all-reduce.15 = (f32[512]{0:T(512)S(1)}, f32[]{:T(128)}) all-reduce(f32[512]{0:T(512)S(1)} %get-tuple-element.210, f32[]{:T(128)} %reduce_sum.422), channel_id=1, replica_groups=mesh['section'=2,'dp'=16] {'dp'}, use_global_device_ids=true, to_apply=%region_31.32 | all-reduce | flops 513 | bytes 4104 | tf_op jit(solution)/shard_map/psum | solution.py:77
  658.5 37.6 %psum.342 = f32[512]{0:T(512)S(1)} all-reduce(f32[512]{0:T(512)S(1)} %fusion.54), channel_id=1, replica_groups=mesh['section'=2,'dp'=16] {'dp'}, use_global_device_ids=true, to_apply=%region_35.36 | all-reduce | flops 512 | bytes 4096 | tf_op jit(solution)/shard_map/psum | solution.py:80
  717.8 37.5 %psum.343 = f32[512]{0:T(512)S(1)} all-reduce(f32[512]{0:T(512)S(1)} %get-tuple-element.212), channel_id=1, replica_groups=mesh['section'=2,'dp'=16] {'dp'}, use_global_device_ids=true, to_apply=%region_38.39 | all-reduce | flops 512 | bytes 4096 | tf_op jit(solution)/shard_map/psum | solution.py:77
  757.6 38.1 %psum.344 = f32[512]{0:T(512)S(1)} all-reduce(f32[512]{0:T(512)S(1)} %fusion.55), channel_id=1, replica_groups=mesh['section'=2,'dp'=16] {'dp'}, use_global_device_ids=true, to_apply=%region_40.41 | all-reduce | flops 512 | bytes 4096 | tf_op jit(solution)/shard_map/psum | solution.py:80
  802.3 37.9 %psum.345 = f32[2048]{0:T(1024)S(1)} all-reduce(f32[2048]{0:T(1024)S(1)} %get-tuple-element.214), channel_id=1, replica_groups=mesh['section'=2,'dp'=16] {'dp'}, use_global_device_ids=true, to_apply=%region_42.43 | all-reduce | flops 2048 | bytes 16384 | tf_op jit(solution)/shard_map/psum | solution.py:77
  844.5 38.3 %psum.346 = f32[2048]{0:T(1024)S(1)} all-reduce(f32[2048]{0:T(1024)S(1)} %fusion.2), channel_id=1, replica_groups=mesh['section'=2,'dp'=16] {'dp'}, use_global_device_ids=true, to_apply=%region_44.45 | all-reduce | flops 2048 | bytes 16384 | tf_op jit(solution)/shard_map/psum | solution.py:80
  907.6 72.4 %all-reduce.14 = (f32[2048]{0:T(1024)S(1)}, f32[2048]{0:T(1024)S(1)}) all-reduce(f32[2048]{0:T(1024)S(1)} %get-tuple-element.16, f32[2048]{0:T(1024)S(1)} %get-tuple-element.15), channel_id=1, replica_groups=mesh['section'=2,'dp'=16] {'dp'}, use_global_device_ids=true, to_apply=%region_48.49 | all-reduce | flops 4096 | bytes 32768 | tf_op jit(solution)/shard_map/psum | solution.py:86
  1058.6 39.2 %all-reduce.12 = (f32[512]{0:T(512)S(1)}, f32[512]{0:T(512)S(1)}) all-reduce(f32[512]{0:T(512)S(1)} %get-tuple-element.26, f32[512]{0:T(512)S(1)} %get-tuple-element.25), channel_id=1, replica_groups=mesh['section'=2,'dp'=16] {'dp'}, use_global_device_ids=true, to_apply=%region_56.57 | all-reduce | flops 1024 | bytes 8192 | tf_op jit(solution)/shard_map/psum | solution.py:86
  1155.8 71.7 %all-reduce.11 = (f32[2048]{0:T(1024)S(1)}, f32[2048]{0:T(1024)S(1)}) all-reduce(f32[2048]{0:T(1024)S(1)} %get-tuple-element.14, f32[2048]{0:T(1024)S(1)} %get-tuple-element.13), channel_id=1, replica_groups=mesh['section'=2,'dp'=16] {'dp'}, use_global_device_ids=true, to_apply=%region_60.61 | all-reduce | flops 4096 | bytes 32768 | tf_op jit(solution)/shard_map/psum | solution.py:86
  1297.9 37.6 %all-reduce.9 = (f32[512]{0:T(512)S(1)}, f32[512]{0:T(512)S(1)}) all-reduce(f32[512]{0:T(512)S(1)} %get-tuple-element.22, f32[512]{0:T(512)S(1)} %get-tuple-element.21), channel_id=1, replica_groups=mesh['section'=2,'dp'=16] {'dp'}, use_global_device_ids=true, to_apply=%region_68.69 | all-reduce | flops 1024 | bytes 8192 | tf_op jit(solution)/shard_map/psum | solution.py:86
  1393.5 72.8 %all-reduce.8 = (f32[2048]{0:T(1024)S(1)}, f32[2048]{0:T(1024)S(1)}) all-reduce(f32[2048]{0:T(1024)S(1)} %get-tuple-element.12, f32[2048]{0:T(1024)S(1)} %get-tuple-element.11), channel_id=1, replica_groups=mesh['section'=2,'dp'=16] {'dp'}, use_global_device_ids=true, to_apply=%region_72.73 | all-reduce | flops 4096 | bytes 32768 | tf_op jit(solution)/shard_map/psum | solution.py:86
  1549.3 39.4 %all-reduce.6 = (f32[512]{0:T(512)S(1)}, f32[512]{0:T(512)S(1)}, f32[48]{0:T(128)S(1)}) all-reduce(f32[512]{0:T(512)S(1)} %get-tuple-element.18, f32[512]{0:T(512)S(1)} %get-tuple-element.17, f32[48]{0:T(128)S(1)} %copy-done.140), channel_id=1, replica_groups=mesh['section'=2,'dp'=16] {'dp'}, use_global_device_ids=true, to_apply=%region_80.81 | all-reduce | flops 1072 | bytes 8576 | tf_op jit(solution)/shard_map/psum | solution.py:86
  1622.2 467.5 %all-reduce.21.cloned.1.call-done = (f32[1,2048,512]{2,1,0:T(8,128)}, f32[1,9,512,512]{3,2,1,0:T(8,128)}, f32[1,512,2048]{2,1,0:T(8,128)}, f32[2048,48]{0,1:T(8,128)}) async-done(((f32[1,2048,512]{2,1,0:T(8,128)}, f32[1,9,512,512]{3,2,1,0:T(8,128)}, f32[1,512,2048]{2,1,0:T(8,128)}, f32[2048,48]{0,1:T(8,128)}), (f32[1,2048,512]{2,1,0:T(8,128)}, f32[1,9,512,512]{3,2,1,0:T(8,128)}, f32[1,512,2048]{2,1,0:T(8,128)}, ...) | async-done | bytes 18219024 | tf_op jit(solution)/shard_map/psum | solution.py:289
  (619 shorter events, 649.8 us)
Async XLA Ops:
  7.2 2082.5 %all-reduce.21.cloned.1.call-start = ((), (), s32[]{:S(2)}) async-start(), calls=%async_computation | async-start | bytes 36438016 | tf_op jit(solution)/shard_map/psum | solution.py:289
  7.2 294.7 %collective-permute-start = (bf16[1,8,96,2048]{3,2,1,0:T(8,128)(2,1)}, bf16[1,8,96,2048]{3,2,1,0:T(8,128)(2,1)}, u32[]{:S(2)}, u32[]{:S(2)}) collective-permute-start(bf16[1,8,96,2048]{3,2,1,0:T(8,128)(2,1)} %param.14), channel_id=1, source_target_pairs={{16,0},{17,1},{18,2},{19,3},{20,4},{21,5},{22,6},{23,7},{24,8},{25... | collective-permute-start | bytes 9437192 | tf_op jit(solution)/shard_map/ppermute | solution.py:35
  102.4 948.4 %copy-start.51 = (f32[1,1,512]{2,1,0:T(1,128)}, f32[1,1,512]{2,1,0:T(1,128)S(1)}, u32[]{:S(2)}) copy-start(f32[1,1,512]{2,1,0:T(1,128)S(1)} %get-tuple-element.180) | copy-start | bytes 6148
  102.5 948.3 %copy-start.58 = (f32[1,1,512]{2,1,0:T(1,128)}, f32[1,1,512]{2,1,0:T(1,128)S(1)}, u32[]{:S(2)}) copy-start(f32[1,1,512]{2,1,0:T(1,128)S(1)} %get-tuple-element.182) | copy-start | bytes 6148
  105.7 7.2 collective-permute-start.1
  109.6 6.5 collective-permute-start.2
  297.9 6.9 collective-permute-start.3
  391.5 6.1 collective-permute-start.4
  394.4 6.5 collective-permute-start.5
  582.9 29.6 %collective-permute-start.7 = (bf16[8,96,2048]{2,1,0:T(8,128)(2,1)}, bf16[8,96,2048]{2,1,0:T(8,128)(2,1)}, u32[]{:S(2)}, u32[]{:S(2)}) collective-permute-start(bf16[8,96,2048]{2,1,0:T(8,128)(2,1)} %bitcast.37), channel_id=1, source_target_pairs={{0,16},{1,17},{2,18},{3,19},{4,20},{5,21},{6,22},{7,23},{8,24},{9,... | collective-permute-start | bytes 9437192 | tf_op jit(solution)/shard_map/ppermute | solution.py:35
  699.3 6.2 collective-permute-start.8
  702.3 6.5 collective-permute-start.9
  1033.4 15.7 collective-permute-start.10
  1037.4 11.6 collective-permute-start.11
  1107.6 23.8 %collective-permute-start.12 = (bf16[8,96,2048]{2,1,0:T(8,128)(2,1)}, bf16[8,96,2048]{2,1,0:T(8,128)(2,1)}, u32[]{:S(2)}, u32[]{:S(2)}) collective-permute-start(bf16[8,96,2048]{2,1,0:T(8,128)(2,1)} %bitcast.66), channel_id=1, source_target_pairs={{16,0},{17,1},{18,2},{19,3},{20,4},{21,5},{22,6},{23,7},{24,8},{25... | collective-permute-start | bytes 9437192 | tf_op jit(solution)/shard_map/ppermute | solution.py:35
  1278.2 8.7 collective-permute-start.13
  1282.0 6.5 collective-permute-start.14
  1343.7 24.4 %collective-permute-start.15 = (bf16[8,96,2048]{2,1,0:T(8,128)(2,1)S(1)}, bf16[8,96,2048]{2,1,0:T(8,128)(2,1)S(1)}, u32[]{:S(2)}, u32[]{:S(2)}) collective-permute-start(bf16[8,96,2048]{2,1,0:T(8,128)(2,1)S(1)} %bitcast.393), channel_id=1, source_target_pairs={{16,0},{17,1},{18,2},{19,3},{20,4},{21,5},{22,6},{23,7},{24,8},{25... | collective-permute-start | bytes 9437192 | tf_op jit(solution)/shard_map/ppermute | solution.py:35
  1516.1 23.8 %collective-permute-start.16 = (bf16[1,96,512]{2,1,0:T(8,128)(2,1)S(1)}, bf16[1,96,512]{2,1,0:T(8,128)(2,1)S(1)}, u32[]{:S(2)}, u32[]{:S(2)}) collective-permute-start(bf16[1,96,512]{2,1,0:T(8,128)(2,1)S(1)} %get-tuple-element.149), channel_id=1, source_target_pairs={{0,1},{1,2},{2,3},{3,4},{4,5},{5,6},{6,7},{7,8},{8,9},{9,10},{10,1... | collective-permute-start | bytes 294920 | tf_op jit(solution)/shard_map/ppermute | solution.py:26
  1520.1 19.7 collective-permute-start.17
  1599.7 20.5 collective-permute-start.18
  1605.9 4.4 collective-permute-start.6
  1612.3 479.6 %collective-permute-start.20 = (bf16[24]{0:T(256)(128)(2,1)S(1)}, bf16[24]{0:T(256)(128)(2,1)S(1)}, u32[]{:S(2)}, u32[]{:S(2)}) collective-permute-start(bf16[24]{0:T(256)(128)(2,1)S(1)} %bitcast.458), channel_id=1, source_target_pairs={{16,0},{17,1},{18,2},{19,3},{20,4},{21,5},{22,6},{23,7},{24,8},{25... | collective-permute-start | bytes 152 | tf_op jit(solution)/shard_map/ppermute | solution.py:35
  2090.7 3.2 collective-permute-start.19
  (169 other events, 5665.9 us)
Sparse Core Ops, SparseCore 0:
  1599.8 489.8 all-reduce.20
where the time goes:
time: 2130 us; the launch traced here: 2120 us
  blocking collectives  1130 us (53%)
  waiting for transfers between devices  489 us (23%)
  matrix products  252 us (12%)
  other arithmetic  136 us (6%)
  starting transfers between devices  48 us (2%)
  local copies, waits for them, and re-layouts  45.7 us (2%)
    psum x1, waiting for transfers between devices, local(): lax.psum((reduce_sum, spatial_sum, expand_sum, head_w_sum, head_b_sum), '...  467 us
    psum x9, blocking collectives, norm_backward(): lax.psum((jnp.sum(upstream, axis=0), jnp.sum(upstream * normed, axis=0)),...  444 us
    psum x9, blocking collectives, norm_forward(): lax.psum((jnp.sum(values * weights, axis=0), local_count), 'dp')  347 us
    psum x9, blocking collectives, norm_forward(): lax.psum(jnp.sum(weights * centered * centered, axis=0), 'dp') / count  339 us
    dot_general x9, matrix products, heads_step(): lax.dot_general(target[:, start:start + HEAD_OUT], head_weight[:, start:s...  93.6 us
  transfers between devices with their start and end apart: 22, of which 10 were waited for; matrix products, arithmetic and copies ran while one was open for 8% of the time, Pallas kernels for 0%

commit v1 on v0

v1 whole, which is shorter than its diff:
```python
import functools
import math

import jax
import jax.numpy as jnp
from jax import lax
from jax.experimental import pallas as pl
from jax.experimental.pallas import tpu as pltpu
from jax.sharding import PartitionSpec as P

TASKS = 3
HEAD_OUT = 16

EPS = 1e-05
SOFT = 0.05
SHARP = 0.1
LEVELS = 1024.0
ACROSS = (((0,), (0,)), ((), ()))
BESIDE = (((1,), (1,)), ((), ()))
MESH = pl.DeviceIdType.MESH
TILE = 512
LIMIT = 56 * 2**20


def grid_of(size):
    side = math.isqrt(size // 4)
    assert side * side * 4 == size
    return (4, side, side)


def greet_all(size):
    section, me = lax.axis_index("section"), lax.axis_index("dp")
    barrier = pltpu.get_barrier_semaphore()
    for step in range(1, size):
        pl.semaphore_signal(
            barrier, inc=1, device_id=(section, lax.rem(me + step, size)), device_id_type=MESH
        )
    pl.semaphore_wait(barrier, size - 1)


def gather_kernel(size, x_ref, o_ref, send_sem, recv_sem):
    section, me = lax.axis_index("section"), lax.axis_index("dp")
    greet_all(size)
    o_ref[0] = x_ref[...]
    copies = []
    for step in range(1, size):
        copy = pltpu.make_async_remote_copy(
            src_ref=x_ref,
            dst_ref=o_ref.at[step],
            send_sem=send_sem.at[step],
            recv_sem=recv_sem.at[step],
            device_id=(section, lax.rem(me + step, size)),
            device_id_type=MESH,
        )
        copy.start()
        copies.append(copy)
    for copy in copies:
        copy.wait()


def gather_stats(values, collective):
    size = lax.axis_size("dp")
    return pl.pallas_call(
        functools.partial(gather_kernel, size),
        out_shape=jax.ShapeDtypeStruct((size,) + values.shape, values.dtype),
        in_specs=[pl.BlockSpec(memory_space=pltpu.VMEM)],
        out_specs=pl.BlockSpec(memory_space=pltpu.VMEM),
        scratch_shapes=[
            pltpu.SemaphoreType.DMA((size,)),
            pltpu.SemaphoreType.DMA((size,)),
        ],
        compiler_params=pltpu.CompilerParams(collective_id=collective, has_side_effects=True),
    )(values)


class Reducer:
    STAGES = 9
    RING = 4

    def __init__(self, size, groups):
        self.size = size
        self.groups = groups
        self.nz, self.ny, self.nx = grid_of(size)
        self.half = TILE // 2
        self.cols = TILE // self.nx
        self.yrows = self.half // self.ny
        self.zrows = self.yrows // self.nz

    def scratch(self):
        nx, ny, nz, groups, cols = self.nx, self.ny, self.nz, self.groups, self.cols
        bf16 = jnp.bfloat16
        return [
            pltpu.VMEM((3 * self.RING, nx, self.half, cols), bf16),
            pltpu.VMEM((3 * groups, nx, self.half, cols), bf16),
            pltpu.VMEM((3 * groups, nx, self.half, cols), bf16),
            pltpu.VMEM((2 * groups, nx - 1, self.half, cols), bf16),
            pltpu.VMEM((2 * groups, ny - 1, self.yrows, cols), bf16),
            pltpu.VMEM((2 * groups, nz - 1, self.zrows, cols), bf16),
            pltpu.VMEM((groups, ny - 1, nx, self.yrows, cols), bf16),
            pltpu.VMEM((groups, nz - 1, nx, self.zrows, cols), bf16),
            pltpu.VMEM((groups, nx - 1, self.zrows, cols), bf16),
            pltpu.SemaphoreType.DMA((3 * groups, 2)),
            pltpu.SemaphoreType.DMA((3 * groups, 2)),
            pltpu.SemaphoreType.DMA((3 * groups, 2 * (nx + ny + nz - 3))),
            pltpu.SemaphoreType.DMA((3 * groups, 2 * (nx + ny + nz - 3))),
        ]

    def bind(self, parts, total, scratch):
        self.parts, self.total = parts, total
        (
            self.ring,
            self.res,
            self.sec,
            self.ax,
            self.ay,
            self.az,
            self.by,
            self.bz,
            self.bx,
            self.pair_send,
            self.pair_recv,
            self.send_sem,
            self.recv_sem,
        ) = scratch
        self.section, self.me = lax.axis_index("section"), lax.axis_index("dp")
        plane = self.ny * self.nx
        self.z = self.me // plane
        self.y = (self.me // self.nx) % self.ny
        self.x = self.me % self.nx

    def peers(self):
        found = [(1 - self.section, self.me)]
        for axis in "xyz":
            for step in range(1, self.count(axis)):
                found.append((self.section, self.other(axis, step)[0]))
        return found

    def greet(self):
        barrier = pltpu.get_barrier_semaphore()
        peers = self.peers()
        for peer in peers:
            pl.semaphore_signal(barrier, inc=1, device_id=peer, device_id_type=MESH)
        pl.semaphore_wait(barrier, len(peers))

    def count(self, axis):
        return {"x": self.nx, "y": self.ny, "z": self.nz}[axis]

    def other(self, axis, step):
        plane = self.ny * self.nx
        if axis == "x":
            place = (self.x + step) % self.nx
            return self.z * plane + self.y * self.nx + place, place
        if axis == "y":
            place = (self.y + step) % self.ny
            return self.z * plane + place * self.nx + self.x, place
        place = (self.z + step) % self.nz
        return place * plane + self.y * self.nx + self.x, place

    def sem(self, axis, back, step):
        base = {"x": 0, "y": self.nx - 1, "z": self.nx + self.ny - 2}[axis]
        return base + (step - 1) + (self.nx + self.ny + self.nz - 3 if back else 0)

    def acc(self, tile):
        return self.ring.at[lax.rem(tile, 3 * self.RING)]

    def block(self, base, x, y, z):
        xs = slice(None) if x is None else x
        if y is None:
            return base.at[xs]
        if z is None:
            return base.at[xs, pl.ds(pl.multiple_of(y * self.yrows, 16), self.yrows)]
        start = pl.multiple_of(y * self.yrows + z * self.zrows, 16)
        return base.at[xs, pl.ds(start, self.zrows)]

    def spread(self, tile, axis, back, source, target):
        copies = []
        for step in range(1, self.count(axis)):
            device, place = self.other(axis, step)
            index = self.sem(axis, back, step)
            copies.append(
                pltpu.make_async_remote_copy(
                    src_ref=source(place),
                    dst_ref=target(step),
                    send_sem=self.send_sem.at[tile, index],
                    recv_sem=self.recv_sem.at[tile, index],
                    device_id=(self.section, device),
                    device_id_type=MESH,
                )
            )
        return copies

    def add(self, ref, extra, target=None):
        total = ref[...].astype(jnp.float32)
        for one in extra:
            total = total + one[...].astype(jnp.float32)
        target = ref if target is None else target
        target[...] = total.astype(jnp.bfloat16)

    def order(self, slot):
        return "xyz" if slot < 2 else "yzx"

    def landing(self, group, slot, axis):
        if slot < 2:
            row = 2 * group + slot
            return {"x": self.ax, "y": self.ay, "z": self.az}[axis].at[row]
        return {"x": self.bx, "y": self.by, "z": self.bz}[axis].at[group]

    def where(self, done, extra=None):
        place = {"x": None, "y": None, "z": None}
        for axis in done:
            place[axis] = {"x": self.x, "y": self.y, "z": self.z}[axis]
        place.update(extra or {})
        return place

    def part(self, base, done, extra=None):
        place = self.where(done, extra)
        return self.block(base, place["x"], place["y"], place["z"])

    def half_rows(self, which):
        return pl.ds(pl.multiple_of(which * self.half, 16), self.half)

    def pair(self, tile):
        own = pltpu.make_async_copy(
            self.parts.at[tile, :, self.half_rows(self.section)],
            self.acc(tile),
            self.pair_send.at[tile, 0],
        )
        away = pltpu.make_async_remote_copy(
            src_ref=self.parts.at[tile, :, self.half_rows(1 - self.section)],
            dst_ref=self.sec.at[tile],
            send_sem=self.pair_send.at[tile, 1],
            recv_sem=self.pair_recv.at[tile, 0],
            device_id=(1 - self.section, self.me),
            device_id_type=MESH,
        )
        return own, away

    def scatter(self, group, slot, level):
        tile = 3 * group + slot
        order = self.order(slot)
        axis, done = order[level], order[:level]
        landing = self.landing(group, slot, axis)
        return self.spread(
            tile,
            axis,
            False,
            lambda place: self.part(self.acc(tile), done, {axis: place}),
            lambda step: landing.at[step - 1],
        )

    def scattered(self, group, slot, level):
        tile = 3 * group + slot
        order = self.order(slot)
        axis, done = order[level], order[: level + 1]
        landing = self.landing(group, slot, axis)
        steps = range(1, self.count(axis))
        for copy in self.scatter(group, slot, level):
            copy.wait()
        target = self.part(self.res.at[tile], done) if level == 2 else None
        self.add(self.part(self.acc(tile), done), [landing.at[step - 1] for step in steps], target)

    def gather(self, group, slot, level):
        tile = 3 * group + slot
        order = self.order(slot)
        axis, done = order[level], order[: level + 1]
        ref = self.part(self.res.at[tile], done)
        return self.spread(tile, axis, True, lambda place: ref, lambda step: ref)

    def gathered(self, group, slot, level):
        for copy in self.gather(group, slot, level):
            copy.wait()

    def final(self, group, slot):
        tile = 3 * group + slot
        block = 1 - (tile >= 3 * self.groups // 2).astype(jnp.int32)
        index = tile - (1 - block) * (3 * self.groups // 2)
        target = self.total.at[index, :, self.half_rows(self.section)]
        here = pltpu.make_async_copy(self.res.at[tile], target, self.pair_send.at[tile, 0])
        away = pltpu.make_async_remote_copy(
            src_ref=self.res.at[tile],
            dst_ref=target,
            send_sem=self.pair_send.at[tile, 0],
            recv_sem=self.pair_recv.at[tile, 1],
            device_id=(1 - self.section, self.me),
            device_id_type=MESH,
        )
        return block == self.section, here, away

    def stage(self, number, group):
        for slot in range(3):
            tile = 3 * group + slot
            if number == 0:
                for copy in self.pair(tile):
                    copy.start()
            elif number == 1:
                for copy in self.pair(tile):
                    copy.wait()
                self.add(self.acc(tile), [self.sec.at[tile]])
                for copy in self.scatter(group, slot, 0):
                    copy.start()
            elif number in (2, 3):
                self.scattered(group, slot, number - 2)
                for copy in self.scatter(group, slot, number - 1):
                    copy.start()
            elif number == 4:
                self.scattered(group, slot, 2)
                for copy in self.gather(group, slot, 2):
                    copy.start()
            elif number in (5, 6):
                self.gathered(group, slot, 7 - number)
                for copy in self.gather(group, slot, 6 - number):
                    copy.start()
            elif number == 7:
                self.gathered(group, slot, 0)
                mine, here, away = self.final(group, slot)
                pl.when(mine)(here.start)
                pl.when(jnp.logical_not(mine))(away.start)
            else:
                mine, here, away = self.final(group, slot)

                @pl.when(mine)
                def _():
                    here.wait()
                    away.wait_recv()

                pl.when(jnp.logical_not(mine))(away.wait_send)

    def tick(self, time):
        for number in reversed(range(self.STAGES)):
            group = time - number
            pl.when(jnp.logical_and(group >= 0, group < self.groups))(
                functools.partial(self.stage, number, group)
            )


def reduce_kernel(size, groups, parts, total, *scratch):
    reducer = Reducer(size, groups)
    reducer.bind(parts, total, scratch)
    reducer.greet()

    @pl.loop(0, groups + reducer.STAGES - 1)
    def _(time):
        reducer.tick(time)


def reduce_tiles(parts):
    size = lax.axis_size("dp")
    groups = parts.shape[0] // 3
    reducer = Reducer(size, groups)
    return pl.pallas_call(
        functools.partial(reduce_kernel, size, groups),
        out_shape=jax.ShapeDtypeStruct((parts.shape[0] // 2,) + parts.shape[1:], parts.dtype),
        in_specs=[pl.BlockSpec(memory_space=pl.ANY)],
        out_specs=pl.BlockSpec(memory_space=pl.ANY),
        scratch_shapes=reducer.scratch(),
        compiler_params=pltpu.CompilerParams(
            collective_id=0, has_side_effects=True, vmem_limit_bytes=LIMIT
        ),
    )(parts)


def extended(x):
    size, length = lax.axis_size("dp"), x.shape[0]
    up = [(i, (i + 1) % size) for i in range(size - 1)]
    down = [(j, i) for i, j in up]
    before = lax.ppermute(lax.slice_in_dim(x, length - 1, length), "dp", up)
    after = lax.ppermute(lax.slice_in_dim(x, 0, 1), "dp", down)
    return jnp.concatenate([before, x, after], axis=0)


def silu_slope(values):
    sigma = jax.nn.sigmoid(values)
    return sigma * (1.0 + values * (1.0 - sigma))


def column_masks(starts, width):
    columns = jnp.arange(width, dtype=jnp.int32)
    crop = jnp.sum((columns[:, None] >= starts[None, :]).astype(jnp.int32), axis=1)
    outside = jnp.full((1,), -1, jnp.int32)
    before = jnp.concatenate([outside, crop[:-1]])
    after = jnp.concatenate([crop[1:], outside])
    return [
        (before == crop).astype(jnp.bfloat16),
        jnp.ones((width,), jnp.bfloat16),
        (after == crop).astype(jnp.bfloat16),
    ]


def patches(padded, masks, sign):
    rows = padded.shape[0] - 2
    width = padded.shape[1]
    wide = jnp.pad(padded, ((0, 0), (1, 1), (0, 0)))
    blocks = []
    for row_step in range(3):
        for col_step in range(3):
            top = 1 + sign * (row_step - 1)
            left = 1 + sign * (col_step - 1)
            piece = wide[top : top + rows, left : left + width]
            if col_step != 1:
                piece = piece * masks[1 + sign * (col_step - 1)][None, :, None]
            blocks.append(piece)
    return jnp.concatenate(blocks, axis=2).reshape(rows * width, -1)


def pick(array, index):
    return lax.dynamic_index_in_dim(array, index, 0, keepdims=False)


def norm_forward(values, weights, local_count):
    total = jnp.sum(values * weights, axis=0)
    centered = values - total / local_count
    spread = jnp.sum(weights * centered * centered, axis=0)
    counts = jnp.full_like(total, local_count)
    parts = gather_stats(jnp.stack([total, spread, counts]), 1 if total.shape[0] == TILE else 2)
    totals, spreads, counts = parts[:, 0], parts[:, 1], parts[:, 2]
    count = jnp.sum(counts[:, 0])
    mean = jnp.sum(totals, axis=0) / count
    apart = totals / counts - mean
    variance = (jnp.sum(spreads, axis=0) + jnp.sum(counts * apart * apart, axis=0)) / count
    scale = lax.rsqrt(variance + EPS)
    return ((values - mean) * scale, scale, count)


def norm_backward(upstream, normed, weights, count, gain, scale):
    local = jnp.stack([jnp.sum(upstream, axis=0), jnp.sum(upstream * normed, axis=0)])
    sums = jnp.sum(gather_stats(local, 3 if local.shape[1] == TILE else 4), axis=0)
    bias_sum, gain_sum = sums[0], sums[1]
    result = scale * gain * (upstream - weights * (bias_sum + normed * gain_sum) / count)
    return (result, gain_sum, bias_sum)


def graddrop(task_grads, bits):
    soft = [jnp.sqrt(value * value + SOFT * SOFT) for value in task_grads]
    signed = task_grads[0]
    magnitude = soft[0]
    for index in range(1, len(task_grads)):
        signed = signed + task_grads[index]
        magnitude = magnitude + soft[index]
    purity = 0.5 * (1.0 + signed / magnitude)
    level = (bits.astype(jnp.float32) + 0.5) / LEVELS
    keep = jax.nn.sigmoid((purity - level) / SHARP)
    merged = jnp.zeros_like(purity)
    for value, scale in zip(task_grads, soft):
        upward = 0.5 * (1.0 + value / scale)
        merged = merged + value * (keep * upward + (1.0 - keep) * (1.0 - upward))
    return merged


def layer_forward(layer_in, params, weights, masks):
    reduce_kernel, spatial, expand_kernel, gain_in, bias_in, gain_out, bias_out = params
    rows, width, channels = layer_in.shape
    flat_in = layer_in.reshape(rows * width, channels)
    local_count = jnp.sum(weights)
    first_map = jnp.dot(flat_in, reduce_kernel, preferred_element_type=jnp.float32)
    normed_a, scale_a, count = norm_forward(first_map, weights, local_count)
    act_a = jax.nn.silu(gain_in[0] * normed_a + bias_in[0]).astype(jnp.bfloat16)
    padded = extended(act_a.reshape(rows, width, -1))
    flat = spatial.reshape(-1, spatial.shape[2])
    second_map = jnp.dot(patches(padded, masks, 1), flat, preferred_element_type=jnp.float32)
    normed_b, scale_b, count = norm_forward(second_map, weights, local_count)
    act_b = jax.nn.silu(gain_in[1] * normed_b + bias_in[1]).astype(jnp.bfloat16)
    third_map = jnp.dot(act_b, expand_kernel, preferred_element_type=jnp.float32)
    normed_c, scale_c, count = norm_forward(third_map, weights, local_count)
    output = jax.nn.silu(gain_out * normed_c + bias_out + flat_in.astype(jnp.float32))
    return (
        output,
        (flat_in, normed_a, scale_a, padded, normed_b, scale_b, normed_c, scale_c, count),
    )


def layer_backward(grad_out, kept, params, weights, masks):
    reduce_kernel, spatial, expand_kernel, gain_in, bias_in, gain_out, bias_out = params
    flat_in, normed_a, scale_a, padded, normed_b, scale_b, normed_c, scale_c, count = kept
    rows, width = (padded.shape[0] - 2, padded.shape[1])
    grad_t = grad_out * silu_slope(gain_out * normed_c + bias_out + flat_in.astype(jnp.float32))
    grad_c, gain_c, bias_c = norm_backward(grad_t, normed_c, weights, count, gain_out, scale_c)
    grad_c = grad_c.astype(jnp.bfloat16)
    affine_b = gain_in[1] * normed_b + bias_in[1]
    act_b = jax.nn.silu(affine_b).astype(jnp.bfloat16)
    expand_part = lax.dot_general(act_b, grad_c, ACROSS, preferred_element_type=jnp.float32)
    grad_act_b = lax.dot_general(grad_c, expand_kernel, BESIDE, preferred_element_type=jnp.float32)
    grad_b, gain_b, bias_b = norm_backward(
        grad_act_b * silu_slope(affine_b), normed_b, weights, count, gain_in[1], scale_b
    )
    grad_b = grad_b.astype(jnp.bfloat16)
    spatial_part = lax.dot_general(
        patches(padded, masks, 1), grad_b, ACROSS, preferred_element_type=jnp.float32
    )
    grad_pad = extended(grad_b.reshape(rows, width, -1))
    back = jnp.swapaxes(spatial, 1, 2).reshape(-1, spatial.shape[1])
    grad_act_a = jnp.dot(patches(grad_pad, masks, -1), back, preferred_element_type=jnp.float32)
    affine_a = gain_in[0] * normed_a + bias_in[0]
    grad_a, gain_a, bias_a = norm_backward(
        grad_act_a * silu_slope(affine_a), normed_a, weights, count, gain_in[0], scale_a
    )
    grad_a = grad_a.astype(jnp.bfloat16)
    reduce_part = lax.dot_general(flat_in, grad_a, ACROSS, preferred_element_type=jnp.float32)
    grad_in = (
        lax.dot_general(grad_a, reduce_kernel, BESIDE, preferred_element_type=jnp.float32) + grad_t
    )
    return (
        grad_in.astype(jnp.bfloat16),
        (reduce_part, spatial_part, expand_part),
        (gain_a, gain_b, bias_a, bias_b, gain_c, bias_c),
    )


def heads_step(feature, head_weight, head_bias, cotangent, weights, bits):
    heads = jnp.dot(feature, head_weight, preferred_element_type=jnp.float32) + head_bias
    target = cotangent * weights.astype(jnp.bfloat16)
    weight_part = lax.dot_general(target, feature, ACROSS, preferred_element_type=jnp.float32)
    bias_part = jnp.sum(target.astype(jnp.float32), axis=0)
    task_grads = []
    for task in range(TASKS):
        start = task * HEAD_OUT
        task_grads.append(
            lax.dot_general(
                target[:, start : start + HEAD_OUT],
                head_weight[:, start : start + HEAD_OUT],
                BESIDE,
                preferred_element_type=jnp.float32,
            )
        )
    return (heads, graddrop(task_grads, bits), weight_part, bias_part)


def tiles_of(kernel_parts, small, nx):
    reduce_part, spatial_part, expand_part = kernel_parts
    cols = TILE // nx

    def rows_first(x):
        x = x.astype(jnp.bfloat16).reshape(-1, TILE, nx, cols)
        return jnp.swapaxes(x, 1, 2)

    expand = expand_part.astype(jnp.bfloat16).reshape(TILE, -1, nx, cols)
    return jnp.concatenate(
        [
            jnp.transpose(expand, (1, 2, 0, 3)),
            rows_first(spatial_part),
            rows_first(reduce_part),
            rows_first(small),
        ]
    )


def local(
    canvases,
    crop_starts,
    pixel_mask,
    drop_bits,
    reduce_weight,
    spatial_weight,
    expand_weight,
    inner_gain,
    inner_bias,
    outer_gain,
    outer_bias,
    head_weight,
    head_bias,
    head_cotangent,
):
    section = lax.axis_index("section")
    first = section == 0
    rows, width, channels = canvases.shape[1:]
    inner = reduce_weight.shape[2]
    pixels = rows * width
    head_cols = head_weight.shape[1]
    swap = [(0, 1), (1, 0)]
    own = (
        reduce_weight[0],
        spatial_weight[0],
        expand_weight[0],
        inner_gain[0],
        inner_bias[0],
        outer_gain[0],
        outer_bias[0],
    )
    came = [lax.ppermute(x, "section", swap) for x in own]
    params = [
        [jnp.where(first, x, y) for x, y in zip(own, came)],
        [jnp.where(first, y, x) for x, y in zip(own, came)],
    ]
    weights = pick(pixel_mask, section).reshape(pixels, 1).astype(jnp.float32)
    masks = column_masks(pick(crop_starts, section), width)
    layer_in = canvases[0]
    saved = []
    for layer in range(2):
        output, kept = layer_forward(layer_in, params[layer], weights, masks)
        saved.append(kept)
        feature = output.astype(jnp.bfloat16)
        layer_in = feature.reshape(rows, width, channels)
    cotangent = pick(head_cotangent, section).reshape(pixels, head_cols)
    bits = pick(drop_bits, section).reshape(pixels, channels)
    heads, grad, head_part, head_bias_part = heads_step(
        feature, head_weight, head_bias, cotangent, weights, bits
    )
    only = lax.axis_index("dp") == 0
    nx = grid_of(lax.axis_size("dp"))[2]
    half = channels // 2
    tiles = []
    for layer in (1, 0):
        grad, kernel_parts, norm_parts = layer_backward(
            grad.astype(jnp.float32), saved[layer], params[layer], weights, masks
        )
        mine = head_part[:, layer * half : (layer + 1) * half].reshape(-1, inner)
        row = jnp.pad(head_bias_part, (0, inner - head_cols))[None]
        norms = jnp.concatenate([x.reshape(-1, inner) for x in norm_parts])
        small = jnp.concatenate([mine, row, jnp.where(only, norms, 0.0)])
        small = jnp.pad(small, ((0, TILE - small.shape[0]), (0, 0)))
        tiles.append(tiles_of(kernel_parts, small, nx))
    total = reduce_tiles(jnp.concatenate(tiles))
    total = jnp.swapaxes(total, 1, 2).reshape(-1, TILE, TILE).astype(jnp.float32)
    across = channels // TILE
    taps = spatial_weight.shape[1]
    expand_total = jnp.swapaxes(total[:across], 0, 1).reshape(inner, channels)
    spatial_total = total[across : across + taps]
    reduce_total = total[across + taps : 2 * across + taps].reshape(channels, inner)
    small = total[-1]
    count = head_cols * half // inner
    head_w_out = small[:count].reshape(head_cols, half).T
    cut = head_cols // 2
    head_b_out = jnp.where(first, small[count, :cut], small[count, cut:head_cols])
    norms = small[count + 1 :]
    return (
        heads.reshape(1, rows, width, head_cols),
        grad.reshape(1, rows, width, channels),
        reduce_total[None],
        spatial_total[None],
        expand_total[None],
        norms[0:2][None],
        norms[2:4][None],
        norms[4 : 4 + across].reshape(1, channels),
        norms[4 + across : 4 + 2 * across].reshape(1, channels),
        head_w_out,
        head_b_out,
    )


def solution(mesh):
    placed = (
        P("section", "dp", None, None),
        P(),
        P(None, "dp", None),
        P(None, "dp", None, None),
        P("section", None, None),
        P("section", None, None, None),
        P("section", None, None),
        P("section", None, None),
        P("section", None, None),
        P("section", None),
        P("section", None),
        P(),
        P(),
        P(None, "dp", None, None),
    )
    return jax.shard_map(
        local,
        mesh=mesh,
        in_specs=placed,
        out_specs=(
            P("section", "dp", None, None),
            P("section", "dp", None, None),
            P("section", None, None),
            P("section", None, None, None),
            P("section", None, None),
            P("section", None, None),
            P("section", None, None),
            P("section", None),
            P("section", None),
            P("section", None),
            P("section"),
        ),
        check_vma=False,
    )
```

time: 2130 us -> 902 us (0.42)
  blocking collectives: 1130 us -> 0 us
  waiting for transfers between devices: 489 us -> 6.25 us
  Pallas kernels: 0 us -> 307 us
  local copies, waits for them, and re-layouts: 45.7 us -> 280 us
  matrix products: 252 us -> 151 us
  starting transfers between devices: 48 us -> 21.7 us
    psum x27 -> x0, blocking collectives: 1130 us -> none  [the longest x9 444 us: norm_backward(): lax.psum((jnp.sum(upstream, axis=0), jnp.sum(upstream * normed, axis=0)),...]
    psum x1 -> x0, waiting for transfers between devices: 467 us -> none  [local(): lax.psum((reduce_sum, spatial_sum, expand_sum, head_w_sum, head_b_sum), '...]
    pallas_call x0 -> x13, Pallas kernels: none -> 307 us  [the longest x1 169 us: reduce_tiles(): pl.pallas_call(functools.partial(reduce_kernel, size, groups), out_shape=...]
    dot_general x9 -> x3, matrix products: 93.6 us -> 31.4 us  [heads_step(): lax.dot_general(target[:, start:start + HEAD_OUT], head_weight[:, start:s...]
    concatenate x6 -> x36, local copies, waits for them, and re-layouts: 0.32 us -> 52.4 us  [patches(): return jnp.concatenate(blocks, axis=2).reshape(rows * width, -1)]
    slice x7 -> x27, local copies, waits for them, and re-layouts: 1.7 us -> 46.6 us  [the longest x2 17.9 us: local(): spatial_total = total[across:across + taps]]
    unnamed x391 -> x270, local copies, waits for them, and re-layouts: 42.5 us -> 86 us
    reshape x3 -> x16, local copies, waits for them, and re-layouts: 0.37 us -> 39.9 us  [the longest x7 29.1 us: rows_first(): x = x.astype(jnp.bfloat16).reshape(-1, TILE, nx, cols)]
  transfers between devices with their start and end apart: 22 -> 15, of which waited for: 10 -> 2; matrix products, arithmetic and copies ran while one was open for 8% -> 17% of each run, Pallas kernels for 0% -> 4%
where the time goes in v1:
time: 902 us; the launch traced here: 892 us
  Pallas kernels  307 us (34%)
  local copies, waits for them, and re-layouts  280 us (31%)
  matrix products  151 us (17%)
  other arithmetic  122 us (14%)
  starting transfers between devices  21.7 us (2%)
    pallas_call x1, Pallas kernels, reduce_tiles(): pl.pallas_call(functools.partial(reduce_kernel, size, groups), out_shape=...  169 us
    pallas_call x12, Pallas kernels, gather_stats(): pl.pallas_call(functools.partial(gather_kernel, size), out_shape=jax.Shap...  138 us
    unnamed x270, local copies, waits for them, and re-layouts  86 us
    concatenate x36, local copies, waits for them, and re-layouts, patches(): return jnp.concatenate(blocks, axis=2).reshape(rows * width, -1)  52.4 us
    dot_general x3, matrix products, heads_step(): lax.dot_general(target[:, start:start + HEAD_OUT], head_weight[:, start:s...  31.4 us
    reshape x7, local copies, waits for them, and re-layouts, rows_first(): x = x.astype(jnp.bfloat16).reshape(-1, TILE, nx, cols)  29.1 us
    dot_general x2, matrix products, layer_backward(): lax.dot_general(grad_a, reduce_kernel, BESIDE, preferred_element_type=jnp...  20.2 us
    dot_general x2, matrix products, layer_backward(): jnp.dot(patches(grad_pad, masks, -1), back, preferred_element_type=jnp.fl...  18.8 us
  transfers between devices with their start and end apart: 15, of which 2 were waited for; matrix products, arithmetic and copies ran while one was open for 17% of the time, Pallas kernels for 4%

profile of v1, /device:TPU:0, one launch (start us, length us, event | category | flops | bytes accessed | tf_op | source)
XLA Modules:
  0.0 891.6 jit_solution(3451843761891688115)
XLA Ops:
  31.1 12.0 %shard_map.221 = f32[16,3,512]{2,1,0:T(4,128)} custom-call(f32[3,512]{1,0:T(4,128)} %maximum_maximum_fusion.2.x_ref), custom_call_target="tpu_custom_call" | custom-call | tf_op jit(solution)/shard_map/pallas_call | solution.py:63
  91.5 9.0 %multiply_reduce_fusion.9 = (f32[512]{0:T(512)S(1)}, f32[768,512]{0,1:T(8,128)S(1)}) fusion(f32[768]{0:T(1024)S(1)} %convert_element_type.157, bf16[768,4608]{0,1:T(8,128)(2,1)} %copy-done.53, bf16[4608,512]{1,0:T(8,128)(2,1)S(1)} %bitcast.375), kind=kOutput, calls=%fused_computation.98 | convolution fusion | flops 3624664576 | bytes 13374464 | tf_op jit(solution)/shard_map/dot_general | solution.py:459
  102.3 9.9 %shard_map.222 = f32[16,3,512]{2,1,0:T(4,128)} custom-call(f32[3,512]{1,0:T(4,128)} %maximum_maximum_fusion.3.x_ref), custom_call_target="tpu_custom_call" | custom-call | tf_op jit(solution)/shard_map/pallas_call | solution.py:63
  123.3 13.8 %shard_map.223 = f32[16,3,2048]{2,1,0:T(4,128)} custom-call(f32[3,2048]{1,0:T(4,128)} %maximum_maximum_fusion.x_ref), custom_call_target="tpu_custom_call" | custom-call | tf_op jit(solution)/shard_map/pallas_call | solution.py:63
  149.7 12.4 %shard_map.224 = f32[16,3,512]{2,1,0:T(4,128)} custom-call(f32[3,512]{1,0:T(4,128)} %maximum_maximum_fusion.4.x_ref), custom_call_target="tpu_custom_call" | custom-call | tf_op jit(solution)/shard_map/pallas_call | solution.py:63
  227.2 12.7 %shard_map.225 = f32[16,3,512]{2,1,0:T(4,128)} custom-call(f32[3,512]{1,0:T(4,128)} %maximum_maximum_fusion.5.x_ref), custom_call_target="tpu_custom_call" | custom-call | tf_op jit(solution)/shard_map/pallas_call | solution.py:63
  251.6 12.2 %shard_map.226 = f32[16,3,2048]{2,1,0:T(4,128)} custom-call(f32[3,2048]{1,0:T(4,128)} %maximum_maximum_fusion.1.x_ref), custom_call_target="tpu_custom_call" | custom-call | tf_op jit(solution)/shard_map/pallas_call | solution.py:63
  268.4 24.1 %fusion.74 = (f32[2048]{0:T(1024)S(1)}, f32[2048]{0:T(1024)S(1)}, f32[768,2048]{1,0:T(8,128)}) fusion(f32[2048]{0:T(1024)S(1)} %get-tuple-element.92, f32[768,2048]{1,0:T(8,128)} %copy-done.3, f32[2048]{0:T(1024)S(1)} %broadcast_divide_fusion, bf16[768,2048]{1,0:T(8,128)(2,1)S(1)} %copy-done.10, f32[2048]{0:T(1024)S(1)} %get-tuple-element.175, ...), kind=kOutput, calls=%fused_computation.334 | convolution fusion | flops 147845120 | bytes 34742272 | tf_op jit(solution)/shard_map/dot_general | solution.py:517
  293.2 11.2 %shard_map.227 = f32[16,2,2048]{2,1,0:T(2,128)} custom-call(f32[2,2048]{1,0:T(2,128)} %pad_maximum_fusion.10.x_ref), custom_call_target="tpu_custom_call" | custom-call | tf_op jit(solution)/shard_map/pallas_call | solution.py:63
  305.5 8.8 multiply_convert_fusion.1
  323.7 9.6 %shard_map.228 = f32[16,2,512]{2,1,0:T(2,128)} custom-call(f32[2,512]{1,0:T(2,128)} %pad_maximum_fusion.12.x_ref), custom_call_target="tpu_custom_call" | custom-call | tf_op jit(solution)/shard_map/pallas_call | solution.py:63
  414.6 8.8 fusion.77
  424.0 11.6 %shard_map.229 = f32[16,2,512]{2,1,0:T(2,128)} custom-call(f32[2,512]{1,0:T(2,128)} %pad_maximum_fusion.13.x_ref), custom_call_target="tpu_custom_call" | custom-call | tf_op jit(solution)/shard_map/pallas_call | solution.py:63
  443.7 11.7 %fusion.73 = (f32[2048]{0:T(1024)S(1)}, f32[2048]{0:T(1024)S(1)}, f32[768,2048]{1,0:T(8,128)}) fusion(f32[2048]{0:T(1024)S(1)} %copy-done.55, f32[768,2048]{1,0:T(8,128)} %copy-done.2, f32[2048]{0:T(1024)S(1)} %copy-done.52, bf16[768,2048]{1,0:T(8,128)(2,1)S(1)} %bitcast.425, f32[2048]{0:T(1024)S(1)} %copy-done.64, f32[2048]{0:T(1024)S(1)} %copy-done.58, ...), kind=kOutput, calls=%fused_computation.333 | convolution fusion | flops 1646653440 | bytes 29422596 | tf_op jit(solution)/shard_map/dot_general | solution.py:499
  456.0 10.5 %shard_map.230 = f32[16,2,2048]{2,1,0:T(2,128)} custom-call(f32[2,2048]{1,0:T(2,128)} %pad_maximum_fusion.11.x_ref), custom_call_target="tpu_custom_call" | custom-call | tf_op jit(solution)/shard_map/pallas_call | solution.py:63
  482.0 9.1 %shard_map.231 = f32[16,2,512]{2,1,0:T(2,128)} custom-call(f32[2,512]{1,0:T(2,128)} %pad_maximum_fusion.14.x_ref), custom_call_target="tpu_custom_call" | custom-call | tf_op jit(solution)/shard_map/pallas_call | solution.py:63
  495.2 8.6 convolution_convert_fusion
  560.0 10.1 %fusion.75 = (f32[512]{0:T(512)S(1)}, f32[512]{0:T(512)S(1)}, f32[768,512]{0,1:T(8,128)}) fusion(f32[512]{0:T(512)S(1)} %copy-done.62, f32[512,768]{1,0:T(8,128)S(1)} %copy-done.6, f32[512]{0:T(512)S(1)} %copy-done.60, f32[512]{0:T(512)S(1)} %bitcast.459, f32[512]{0:T(512)S(1)} %bitcast.453, bf16[768,4608]{0,1:T(8,128)(2,1)} %constant_dynamic-update-slice_fusion.27, ...), kind=kOutput, calls=%fused_computation.335 | convolution fusion | flops 3629775872 | bytes 14954496 | tf_op jit(solution)/shard_map/dot_general | solution.py:491
  570.6 12.6 %shard_map.232 = f32[16,2,512]{2,1,0:T(2,128)} custom-call(f32[2,512]{1,0:T(2,128)} %pad_maximum_fusion.15.x_ref), custom_call_target="tpu_custom_call" | custom-call | tf_op jit(solution)/shard_map/pallas_call | solution.py:63
  612.3 169.3 %shard_map.233 = bf16[18,2,512,256]{3,2,1,0:T(8,128)(2,1)} custom-call(bf16[36,2,512,256]{3,2,1,0:T(8,128)(2,1)} %bitcast_dynamic-update-slice_fusion.6.parts), custom_call_target="tpu_custom_call" | custom-call | tf_op jit(solution)/shard_map/pallas_call | solution.py:350
  781.6 12.6 %convert_bitcast_fusion = f32[18,512,2,256]{3,1,2,0:T(8,128)} fusion(bf16[18,2,512,256]{3,2,1,0:T(8,128)(2,1)} %shard_map.233), kind=kLoop, calls=%fused_computation | loop fusion | flops 4718592 | bytes 28311552 | tf_op jit(solution)/shard_map/convert_element_type | solution.py:612
  802.5 18.7 %copy.355 = f32[18,512,2,256]{1,3,2,0:T(8,128)} copy(f32[18,512,2,256]{3,1,2,0:T(8,128)} %convert_bitcast_fusion) | data formatting | bytes 37748736 | tf_op jit(solution)/shard_map/convert_element_type | solution.py:612
  832.3 9.7 %copy.353 = f32[9,512,2,256]{1,3,2,0:T(8,128)} copy(f32[9,512,2,256]{3,1,2,0:T(8,128)} %slice.592) | data formatting | bytes 18874368 | tf_op jit(solution)/shard_map/slice | solution.py:616
  842.0 9.8 %copy.361 = f32[1,9,512,512]{3,2,1,0:T(8,128)} copy(f32[1,9,512,512]{2,3,1,0:T(8,128)} %bitcast.369) | data formatting | bytes 18874368
  (528 shorter events, 450.2 us)
Async XLA Ops:
  0.7 22.9 %collective-permute-start.2 = (bf16[2048,512]{1,0:T(8,128)(2,1)}, bf16[2048,512]{1,0:T(8,128)(2,1)S(1)}, u32[]{:S(2)}, u32[]{:S(2)}) collective-permute-start(bf16[2048,512]{1,0:T(8,128)(2,1)} %bitcast.522), channel_id=1, source_target_pairs={{0,16},{16,0},{1,17},{17,1},{2,18},{18,2},{3,19},{19,3},{4,20},{20... | collective-permute-start | bytes 6291464 | tf_op jit(solution)/shard_map/ppermute | solution.py:578
  1.2 20.0 %collective-permute-start.1 = (f32[2,512]{1,0:T(2,128)}, f32[2,512]{1,0:T(2,128)S(1)}, u32[]{:S(2)}, u32[]{:S(2)}) collective-permute-start(f32[2,512]{1,0:T(2,128)} %bitcast.496), channel_id=1, source_target_pairs={{0,16},{16,0},{1,17},{17,1},{2,18},{18,2},{3,19},{19,3},{4,20},{20... | collective-permute-start | bytes 12296 | tf_op jit(solution)/shard_map/ppermute | solution.py:578
  1.3 20.0 %collective-permute-start.3 = (f32[2,512]{1,0:T(2,128)}, f32[2,512]{1,0:T(2,128)S(1)}, u32[]{:S(2)}, u32[]{:S(2)}) collective-permute-start(f32[2,512]{1,0:T(2,128)} %bitcast.495), channel_id=1, source_target_pairs={{0,16},{16,0},{1,17},{17,1},{2,18},{18,2},{3,19},{19,3},{4,20},{20... | collective-permute-start | bytes 12296 | tf_op jit(solution)/shard_map/ppermute | solution.py:578
  1.7 83.3 %collective-permute-start.6 = (bf16[9,512,512]{2,1,0:T(8,128)(2,1)}, bf16[9,512,512]{2,1,0:T(8,128)(2,1)}, u32[]{:S(2)}, u32[]{:S(2)}) collective-permute-start(bf16[9,512,512]{2,1,0:T(8,128)(2,1)} %bitcast.390), channel_id=1, source_target_pairs={{0,16},{16,0},{1,17},{17,1},{2,18},{18,2},{3,19},{19,3},{4,20},{20... | collective-permute-start | bytes 14155784 | tf_op jit(solution)/shard_map/ppermute | solution.py:578
  1.8 114.1 %collective-permute-start.7 = (bf16[512,2048]{1,0:T(8,128)(2,1)}, bf16[512,2048]{1,0:T(8,128)(2,1)}, u32[]{:S(2)}, u32[]{:S(2)}) collective-permute-start(bf16[512,2048]{1,0:T(8,128)(2,1)} %bitcast.521), channel_id=1, source_target_pairs={{0,16},{16,0},{1,17},{17,1},{2,18},{18,2},{3,19},{19,3},{4,20},{20... | collective-permute-start | bytes 6291464 | tf_op jit(solution)/shard_map/ppermute | solution.py:578
  21.2 119.0 %collective-permute-start = (f32[2048]{0:T(1024)S(1)}, f32[2048]{0:T(1024)}, u32[]{:S(2)}, u32[]{:S(2)}) collective-permute-start(f32[2048]{0:T(1024)S(1)} %bitcast.444), channel_id=1, source_target_pairs={{0,16},{16,0},{1,17},{17,1},{2,18},{18,2},{3,19},{19,3},{4,20},{20... | collective-permute-start | bytes 24584 | tf_op jit(solution)/shard_map/ppermute | solution.py:578
  21.3 29.8 %collective-permute-start.8 = (f32[2048]{0:T(1024)S(1)}, f32[2048]{0:T(1024)S(1)}, u32[]{:S(2)}, u32[]{:S(2)}) collective-permute-start(f32[2048]{0:T(1024)S(1)} %bitcast.489), channel_id=1, source_target_pairs={{0,16},{16,0},{1,17},{17,1},{2,18},{18,2},{3,19},{19,3},{4,20},{20... | collective-permute-start | bytes 24584 | tf_op jit(solution)/shard_map/ppermute | solution.py:578
  21.7 57.7 %copy-start.66 = (f32[1,512]{1,0:T(1,128)}, f32[1,512]{1,0:T(1,128)S(1)}, u32[]{:S(2)}) copy-start(f32[1,512]{1,0:T(1,128)S(1)} %slice.531) | copy-start | bytes 6148
  29.4 50.1 %copy-start.5 = (f32[512,768]{1,0:T(8,128)}, f32[512,768]{1,0:T(8,128)S(1)}, u32[]{:S(2)}) copy-start(f32[512,768]{1,0:T(8,128)S(1)} %get-tuple-element.204) | copy-start | bytes 4718596
  45.5 34.0 %copy-start.59 = (f32[512]{0:T(512)}, f32[512]{0:T(512)S(1)}, u32[]{:S(2)}) copy-start(f32[512]{0:T(512)S(1)} %broadcast_divide_fusion.7) | copy-start | bytes 6148
  46.2 69.1 %copy-start.61 = (f32[512]{0:T(512)}, f32[512]{0:T(512)S(1)}, u32[]{:S(2)}) copy-start(f32[512]{0:T(512)S(1)} %add_rsqrt_fusion.5) | copy-start | bytes 6148
  47.6 6.8 collective-permute-start.4
  51.1 8.1 collective-permute-start.5
  52.6 88.8 %copy-start.63 = (f32[2048]{0:T(1024)}, f32[2048]{0:T(1024)S(1)}, u32[]{:S(2)}) copy-start(f32[2048]{0:T(1024)S(1)} %get-tuple-element.176) | copy-start | bytes 24580
  91.5 24.4 %copy-start.98 = (f32[1,512]{1,0:T(1,128)S(1)}, f32[1,512]{1,0:T(1,128)}, u32[]{:S(2)}) copy-start(f32[1,512]{1,0:T(1,128)} %get-tuple-element.197) | copy-start | bytes 6148
  147.9 59.8 %copy-start.7 = (f32[768,512]{0,1:T(8,128)}, f32[768,512]{0,1:T(8,128)S(1)}, u32[]{:S(2)}) copy-start(f32[768,512]{0,1:T(8,128)S(1)} %get-tuple-element.210) | copy-start | bytes 4718596
  166.6 19.5 %collective-permute-start.9 = (bf16[1,96,512]{1,2,0:T(8,128)(2,1)}, bf16[1,96,512]{1,2,0:T(8,128)(2,1)S(1)}, u32[]{:S(2)}, u32[]{:S(2)}) collective-permute-start(bf16[1,96,512]{1,2,0:T(8,128)(2,1)} %get-tuple-element.149), channel_id=1, source_target_pairs={{0,1},{1,2},{2,3},{3,4},{4,5},{5,6},{6,7},{7,8},{8,9},{9,10},{10,1... | collective-permute-start | bytes 294920 | tf_op jit(solution)/shard_map/ppermute | solution.py:366
  170.1 16.2 %collective-permute-start.10 = (bf16[1,96,512]{1,2,0:T(8,128)(2,1)}, bf16[1,96,512]{1,2,0:T(8,128)(2,1)S(1)}, u32[]{:S(2)}, u32[]{:S(2)}) collective-permute-start(bf16[1,96,512]{1,2,0:T(8,128)(2,1)} %get-tuple-element.150), channel_id=1, source_target_pairs={{1,0},{2,1},{3,2},{4,3},{5,4},{6,5},{7,6},{8,7},{9,8},{10,9},{11,1... | collective-permute-start | bytes 294920 | tf_op jit(solution)/shard_map/ppermute | solution.py:367
  217.3 26.4 %copy-start.100 = (f32[1,512]{1,0:T(1,128)S(1)}, f32[1,512]{1,0:T(1,128)}, u32[]{:S(2)}) copy-start(f32[1,512]{1,0:T(1,128)} %get-tuple-element.195) | copy-start | bytes 6148
  347.4 35.4 %collective-permute-start.11 = (bf16[1,96,512]{1,2,0:T(8,128)(2,1)}, bf16[1,96,512]{1,2,0:T(8,128)(2,1)}, u32[]{:S(2)}, u32[]{:S(2)}) collective-permute-start(bf16[1,96,512]{1,2,0:T(8,128)(2,1)} %get-tuple-element.145), channel_id=1, source_target_pairs={{0,1},{1,2},{2,3},{3,4},{4,5},{5,6},{6,7},{7,8},{8,9},{9,10},{10,1... | collective-permute-start | bytes 294920 | tf_op jit(solution)/shard_map/ppermute | solution.py:366
  351.4 32.4 %collective-permute-start.12 = (bf16[1,96,512]{1,2,0:T(8,128)(2,1)}, bf16[1,96,512]{1,2,0:T(8,128)(2,1)}, u32[]{:S(2)}, u32[]{:S(2)}) collective-permute-start(bf16[1,96,512]{1,2,0:T(8,128)(2,1)} %get-tuple-element.146), channel_id=1, source_target_pairs={{1,0},{2,1},{3,2},{4,3},{5,4},{6,5},{7,6},{8,7},{9,8},{10,9},{11,1... | collective-permute-start | bytes 294920 | tf_op jit(solution)/shard_map/ppermute | solution.py:367
  503.8 28.7 %collective-permute-start.13 = (bf16[1,96,512]{1,2,0:T(8,128)(2,1)S(1)}, bf16[1,96,512]{1,2,0:T(8,128)(2,1)S(1)}, u32[]{:S(2)}, u32[]{:S(2)}) collective-permute-start(bf16[1,96,512]{1,2,0:T(8,128)(2,1)S(1)} %get-tuple-element.141), channel_id=1, source_target_pairs={{0,1},{1,2},{2,3},{3,4},{4,5},{5,6},{6,7},{7,8},{8,9},{9,10},{10,1... | collective-permute-start | bytes 294920 | tf_op jit(solution)/shard_map/ppermute | solution.py:366
  506.7 25.9 %collective-permute-start.14 = (bf16[1,96,512]{1,2,0:T(8,128)(2,1)S(1)}, bf16[1,96,512]{1,2,0:T(8,128)(2,1)S(1)}, u32[]{:S(2)}, u32[]{:S(2)}) collective-permute-start(bf16[1,96,512]{1,2,0:T(8,128)(2,1)S(1)} %get-tuple-element.142), channel_id=1, source_target_pairs={{1,0},{2,1},{3,2},{4,3},{5,4},{6,5},{7,6},{8,7},{9,8},{10,9},{11,1... | collective-permute-start | bytes 294920 | tf_op jit(solution)/shard_map/ppermute | solution.py:367
  560.0 24.2 %copy-start.94 = (f32[1,512]{1,0:T(1,128)S(1)}, f32[1,512]{1,0:T(1,128)}, u32[]{:S(2)}) copy-start(f32[1,512]{1,0:T(1,128)} %get-tuple-element.181) | copy-start | bytes 6148
  (102 other events, 663.7 us)

commit v2 on v1

v2 whole, which is shorter than its diff:
```python
import functools
import math

import jax
import jax.numpy as jnp
from jax import lax
from jax.experimental import pallas as pl
from jax.experimental.pallas import tpu as pltpu
from jax.sharding import PartitionSpec as P

TASKS = 3
HEAD_OUT = 16

EPS = 1e-05
SOFT = 0.05
SHARP = 0.1
LEVELS = 1024.0
ACROSS = (((0,), (0,)), ((), ()))
BESIDE = (((1,), (1,)), ((), ()))
MESH = pl.DeviceIdType.MESH
TILE = 512
LIMIT = 56 * 2**20


def grid_of(size):
    side = math.isqrt(size // 4)
    assert side * side * 4 == size
    return (4, side, side)


class Reducer:
    STAGES = 9
    RING = 4

    def __init__(self, size, groups):
        self.size = size
        self.groups = groups
        self.nz, self.ny, self.nx = grid_of(size)
        self.half = TILE // 2
        self.cols = TILE // self.nx
        self.yrows = self.half // self.ny
        self.zrows = self.yrows // self.nz

    def scratch(self):
        nx, ny, nz, groups, cols = self.nx, self.ny, self.nz, self.groups, self.cols
        bf16 = jnp.bfloat16
        return [
            pltpu.VMEM((3 * self.RING, self.half, TILE), bf16),
            pltpu.VMEM((3 * groups, self.half, TILE), bf16),
            pltpu.VMEM((3 * groups, self.half, TILE), bf16),
            pltpu.VMEM((2 * groups, nx - 1, self.half, cols), bf16),
            pltpu.VMEM((2 * groups, ny - 1, self.yrows, cols), bf16),
            pltpu.VMEM((2 * groups, nz - 1, self.zrows, cols), bf16),
            pltpu.VMEM((groups, ny - 1, self.yrows, TILE), bf16),
            pltpu.VMEM((groups, nz - 1, self.zrows, TILE), bf16),
            pltpu.VMEM((groups, nx - 1, self.zrows, cols), bf16),
            pltpu.SemaphoreType.DMA((3 * groups, 2)),
            pltpu.SemaphoreType.DMA((3 * groups, 2)),
            pltpu.SemaphoreType.DMA((3 * groups, 2 * (nx + ny + nz - 3))),
            pltpu.SemaphoreType.DMA((3 * groups, 2 * (nx + ny + nz - 3))),
        ]

    def bind(self, parts, total, scratch):
        self.parts, self.total = parts, total
        (
            self.ring,
            self.res,
            self.sec,
            self.ax,
            self.ay,
            self.az,
            self.by,
            self.bz,
            self.bx,
            self.pair_send,
            self.pair_recv,
            self.send_sem,
            self.recv_sem,
        ) = scratch
        self.section, self.me = lax.axis_index("section"), lax.axis_index("dp")
        plane = self.ny * self.nx
        self.z = self.me // plane
        self.y = (self.me // self.nx) % self.ny
        self.x = self.me % self.nx

    def peers(self):
        found = [(1 - self.section, self.me)]
        for axis in "xyz":
            for step in range(1, self.count(axis)):
                found.append((self.section, self.other(axis, step)[0]))
        return found

    def greet(self):
        barrier = pltpu.get_barrier_semaphore()
        peers = self.peers()
        for peer in peers:
            pl.semaphore_signal(barrier, inc=1, device_id=peer, device_id_type=MESH)
        pl.semaphore_wait(barrier, len(peers))

    def count(self, axis):
        return {"x": self.nx, "y": self.ny, "z": self.nz}[axis]

    def other(self, axis, step):
        plane = self.ny * self.nx
        if axis == "x":
            place = (self.x + step) % self.nx
            return self.z * plane + self.y * self.nx + place, place
        if axis == "y":
            place = (self.y + step) % self.ny
            return self.z * plane + place * self.nx + self.x, place
        place = (self.z + step) % self.nz
        return place * plane + self.y * self.nx + self.x, place

    def sem(self, axis, back, step):
        base = {"x": 0, "y": self.nx - 1, "z": self.nx + self.ny - 2}[axis]
        return base + (step - 1) + (self.nx + self.ny + self.nz - 3 if back else 0)

    def acc(self, tile):
        return self.ring.at[lax.rem(tile, 3 * self.RING)]

    def block(self, base, x, y, z):
        if y is None:
            lines = slice(None)
        elif z is None:
            lines = pl.ds(pl.multiple_of(y * self.yrows, 16), self.yrows)
        else:
            lines = pl.ds(pl.multiple_of(y * self.yrows + z * self.zrows, 16), self.zrows)
        if x is None:
            return base.at[lines]
        return base.at[lines, pl.ds(pl.multiple_of(x * self.cols, self.cols), self.cols)]

    def spread(self, tile, axis, back, source, target):
        copies = []
        for step in range(1, self.count(axis)):
            device, place = self.other(axis, step)
            index = self.sem(axis, back, step)
            copies.append(
                pltpu.make_async_remote_copy(
                    src_ref=source(place),
                    dst_ref=target(step),
                    send_sem=self.send_sem.at[tile, index],
                    recv_sem=self.recv_sem.at[tile, index],
                    device_id=(self.section, device),
                    device_id_type=MESH,
                )
            )
        return copies

    def add(self, ref, extra, target=None):
        total = ref[...].astype(jnp.float32)
        for one in extra:
            total = total + one[...].astype(jnp.float32)
        target = ref if target is None else target
        target[...] = total.astype(jnp.bfloat16)

    def order(self, slot):
        return "xyz" if slot < 2 else "yzx"

    def landing(self, group, slot, axis):
        if slot < 2:
            row = 2 * group + slot
            return {"x": self.ax, "y": self.ay, "z": self.az}[axis].at[row]
        return {"x": self.bx, "y": self.by, "z": self.bz}[axis].at[group]

    def where(self, done, extra=None):
        place = {"x": None, "y": None, "z": None}
        for axis in done:
            place[axis] = {"x": self.x, "y": self.y, "z": self.z}[axis]
        place.update(extra or {})
        return place

    def part(self, base, done, extra=None):
        place = self.where(done, extra)
        return self.block(base, place["x"], place["y"], place["z"])

    def half_rows(self, which):
        return pl.ds(pl.multiple_of(which * self.half, 16), self.half)

    def pair(self, tile):
        own = pltpu.make_async_copy(
            self.parts.at[tile, self.half_rows(self.section)],
            self.acc(tile),
            self.pair_send.at[tile, 0],
        )
        away = pltpu.make_async_remote_copy(
            src_ref=self.parts.at[tile, self.half_rows(1 - self.section)],
            dst_ref=self.sec.at[tile],
            send_sem=self.pair_send.at[tile, 1],
            recv_sem=self.pair_recv.at[tile, 0],
            device_id=(1 - self.section, self.me),
            device_id_type=MESH,
        )
        return own, away

    def scatter(self, group, slot, level):
        tile = 3 * group + slot
        order = self.order(slot)
        axis, done = order[level], order[:level]
        landing = self.landing(group, slot, axis)
        return self.spread(
            tile,
            axis,
            False,
            lambda place: self.part(self.acc(tile), done, {axis: place}),
            lambda step: landing.at[step - 1],
        )

    def scattered(self, group, slot, level):
        tile = 3 * group + slot
        order = self.order(slot)
        axis, done = order[level], order[: level + 1]
        landing = self.landing(group, slot, axis)
        steps = range(1, self.count(axis))
        for copy in self.scatter(group, slot, level):
            copy.wait()
        target = self.part(self.res.at[tile], done) if level == 2 else None
        self.add(self.part(self.acc(tile), done), [landing.at[step - 1] for step in steps], target)

    def gather(self, group, slot, level):
        tile = 3 * group + slot
        order = self.order(slot)
        axis, done = order[level], order[: level + 1]
        ref = self.part(self.res.at[tile], done)
        return self.spread(tile, axis, True, lambda place: ref, lambda step: ref)

    def gathered(self, group, slot, level):
        for copy in self.gather(group, slot, level):
            copy.wait()

    def places(self, index):
        expand, spatial, reduce, small = self.total
        across = expand.shape[1] // TILE
        half = self.half_rows(self.section)
        taps = spatial.shape[0]
        tile = index - across - taps
        lines = pl.multiple_of(tile * TILE + self.section * self.half, 16)
        return [
            (index < across, lambda: expand.at[half, pl.ds(pl.multiple_of(index * TILE, TILE), TILE)]),
            (
                jnp.logical_and(index >= across, index < across + taps),
                lambda: spatial.at[index - across, half],
            ),
            (
                jnp.logical_and(index >= across + taps, index < 2 * across + taps),
                lambda: reduce.at[pl.ds(lines, self.half)],
            ),
            (index == 2 * across + taps, lambda: small.at[half]),
        ]

    def final(self, tile, target):
        here = pltpu.make_async_copy(self.res.at[tile], target, self.pair_send.at[tile, 0])
        away = pltpu.make_async_remote_copy(
            src_ref=self.res.at[tile],
            dst_ref=target,
            send_sem=self.pair_send.at[tile, 0],
            recv_sem=self.pair_recv.at[tile, 1],
            device_id=(1 - self.section, self.me),
            device_id_type=MESH,
        )
        return here, away

    def finish(self, tile):
        later = (tile >= 3 * self.groups // 2).astype(jnp.int32)
        mine = self.section == 1 - later
        index = tile - later * (3 * self.groups // 2)
        for wanted, place in self.places(index):

            @pl.when(jnp.logical_and(wanted, mine))
            def _():
                self.final(tile, place())[0].start()

            @pl.when(jnp.logical_and(wanted, jnp.logical_not(mine)))
            def _():
                self.final(tile, place())[1].start()

    def finished(self, tile):
        later = (tile >= 3 * self.groups // 2).astype(jnp.int32)
        mine = self.section == 1 - later
        here, away = self.final(tile, self.total[3].at[self.half_rows(self.section)])

        @pl.when(mine)
        def _():
            here.wait()
            away.wait_recv()

        pl.when(jnp.logical_not(mine))(away.wait_send)

    def stage(self, number, group):
        for slot in range(3):
            tile = 3 * group + slot
            if number == 0:
                for copy in self.pair(tile):
                    copy.start()
            elif number == 1:
                for copy in self.pair(tile):
                    copy.wait()
                self.add(self.acc(tile), [self.sec.at[tile]])
                for copy in self.scatter(group, slot, 0):
                    copy.start()
            elif number in (2, 3):
                self.scattered(group, slot, number - 2)
                for copy in self.scatter(group, slot, number - 1):
                    copy.start()
            elif number == 4:
                self.scattered(group, slot, 2)
                for copy in self.gather(group, slot, 2):
                    copy.start()
            elif number in (5, 6):
                self.gathered(group, slot, 7 - number)
                for copy in self.gather(group, slot, 6 - number):
                    copy.start()
            elif number == 7:
                self.gathered(group, slot, 0)
                self.finish(tile)
            else:
                self.finished(tile)

    def tick(self, time):
        for number in reversed(range(self.STAGES)):
            group = time - number
            pl.when(jnp.logical_and(group >= 0, group < self.groups))(
                functools.partial(self.stage, number, group)
            )


def reduce_kernel(size, groups, parts, expand, spatial, reduce, small, *scratch):
    reducer = Reducer(size, groups)
    reducer.bind(parts, (expand, spatial, reduce, small), scratch)
    reducer.greet()

    @pl.loop(0, groups + reducer.STAGES - 1)
    def _(time):
        reducer.tick(time)


def reduce_tiles(parts, channels, taps):
    size = lax.axis_size("dp")
    groups = parts.shape[0] // 3
    reducer = Reducer(size, groups)
    shapes = [(TILE, channels), (taps, TILE, TILE), (channels, TILE), (TILE, TILE)]
    return pl.pallas_call(
        functools.partial(reduce_kernel, size, groups),
        out_shape=[jax.ShapeDtypeStruct(shape, parts.dtype) for shape in shapes],
        in_specs=[pl.BlockSpec(memory_space=pl.ANY)],
        out_specs=[pl.BlockSpec(memory_space=pl.ANY)] * 4,
        scratch_shapes=reducer.scratch(),
        compiler_params=pltpu.CompilerParams(
            collective_id=0, has_side_effects=True, vmem_limit_bytes=LIMIT
        ),
    )(parts)


def silu_parts(v):
    sigma = 1.0 / (1.0 + jnp.exp(-v))
    return v * sigma, sigma * (1.0 + v * (1.0 - sigma))


def folded(x):
    return jnp.sum(x.reshape(x.shape[0] // 8, 8, x.shape[1]), axis=0)


class Exchange:
    def __init__(self, size, send_sem, recv_sem, edge_send, edge_recv):
        self.size = size
        self.section, self.me = lax.axis_index("section"), lax.axis_index("dp")
        self.send_sem, self.recv_sem = send_sem, recv_sem
        self.edge_send, self.edge_recv = edge_send, edge_recv

    def greet(self):
        barrier = pltpu.get_barrier_semaphore()
        for step in range(1, self.size):
            peer = (self.section, lax.rem(self.me + step, self.size))
            pl.semaphore_signal(barrier, inc=1, device_id=peer, device_id_type=MESH)
        other = (1 - self.section, self.me)
        pl.semaphore_signal(barrier, inc=1, device_id=other, device_id_type=MESH)
        pl.semaphore_wait(barrier, self.size)

    def copies(self, number, slots):
        return [
            pltpu.make_async_remote_copy(
                src_ref=slots.at[0],
                dst_ref=slots.at[step],
                send_sem=self.send_sem.at[number, step],
                recv_sem=self.recv_sem.at[number, step],
                device_id=(self.section, lax.rem(self.me + step, self.size)),
                device_id_type=MESH,
            )
            for step in range(1, self.size)
        ]

    def edges(self, number, first, last, landing):
        made = []
        for way, (ref, step) in enumerate(((first, self.size - 1), (last, 1))):
            made.append(
                pltpu.make_async_remote_copy(
                    src_ref=ref,
                    dst_ref=landing.at[1 - way],
                    send_sem=self.edge_send.at[number, way],
                    recv_sem=self.edge_recv.at[number, 1 - way],
                    device_id=(self.section, lax.rem(self.me + step, self.size)),
                    device_id_type=MESH,
                )
            )
        return made

    def start_edges(self, number, first, last, landing):
        up, down = self.edges(number, first, last, landing)
        pl.when(self.me > 0)(up.start)
        pl.when(self.me < self.size - 1)(down.start)

    def wait_edges(self, number, first, last, landing):
        up, down = self.edges(number, first, last, landing)
        pl.when(self.me > 0)(up.wait_send)
        pl.when(self.me > 0)(down.wait_recv)
        pl.when(self.me < self.size - 1)(down.wait_send)
        pl.when(self.me < self.size - 1)(up.wait_recv)


def forward_kernel(
    size,
    u_hbm,
    bits_hbm,
    cot_hbm,
    wr_hbm,
    ws_hbm,
    we_hbm,
    ig_ref,
    ib_ref,
    og_ref,
    ob_ref,
    hwt_ref,
    hb_ref,
    info_ref,
    heads_ref,
    hwg_ref,
    hbg_ref,
    igs,
    ibs,
    ogs,
    obs,
    rs_ref,
    rc_ref,
    merged_hbm,
    u1_hbm,
    zc_hbm,
    za_hbm,
    zb_hbm,
    r1_hbm,
    wr_all,
    ws_all,
    we_all,
    wr,
    ws,
    we,
    u0,
    u1,
    a_ref,
    b_ref,
    e_ref,
    cat,
    r2,
    za,
    zb,
    zc,
    merged,
    bits,
    cot,
    halo,
    msg,
    msg_c,
    first_msg,
    stat,
    stat_c,
    send_sem,
    recv_sem,
    edge_send,
    edge_recv,
    w_load,
    w_send,
    w_recv,
    w_out,
    in_sem,
    bit_sem,
    out_sem,
):
    link = Exchange(size, send_sem, recv_sem, edge_send, edge_recv)
    section, me = link.section, link.me
    pixels, channels = u0.shape
    inner = a_ref.shape[1]
    rows, width = bits_hbm.shape[1], bits_hbm.shape[2]
    f32, bf16 = jnp.float32, jnp.bfloat16

    load_u = pltpu.make_async_copy(u_hbm, u0, in_sem.at[0])
    load_cot = pltpu.make_async_copy(cot_hbm.at[section], cot, in_sem.at[1])

    def load_bits(chunk):
        return pltpu.make_async_copy(
            bits_hbm.at[section, chunk], bits.at[chunk % 2], bit_sem.at[chunk % 2]
        )

    load_u.start()
    load_cot.start()
    load_bits(0).start()
    load_bits(1).start()

    weights = ((wr_hbm, wr, wr_all), (ws_hbm, ws, ws_all), (we_hbm, we, we_all))

    def local_load(kind):
        source, target, _ = weights[kind]
        return pltpu.make_async_copy(source, target.at[section], w_load.at[kind])

    def pushed(kind):
        source, target, _ = weights[kind]
        return pltpu.make_async_remote_copy(
            src_ref=source,
            dst_ref=target.at[section],
            send_sem=w_send.at[kind],
            recv_sem=w_recv.at[kind],
            device_id=(1 - section, me),
            device_id_type=MESH,
        )

    vectors = ((ig_ref, igs), (ib_ref, ibs), (og_ref, ogs), (ob_ref, obs))

    def pushed_vector(kind):
        source, target = vectors[kind]
        return pltpu.make_async_remote_copy(
            src_ref=source,
            dst_ref=target.at[section],
            send_sem=w_send.at[3 + kind],
            recv_sem=w_recv.at[3 + kind],
            device_id=(1 - section, me),
            device_id_type=MESH,
        )

    def save_weight(kind, layer):
        _, target, saved = weights[kind]
        return pltpu.make_async_copy(target.at[layer], saved.at[layer], w_out.at[kind, layer])

    for kind in range(3):
        local_load(kind).start()
    link.greet()
    for kind in range(4):
        pushed_vector(kind).start()
    for kind in range(3):
        pushed(kind).start()
    for source, target in vectors:
        target[section] = source[...]

    def need_weight(kind, layer):
        pl.when(section == layer)(local_load(kind).wait)
        pl.when(section != layer)(pushed(kind).wait_recv)
        save_weight(kind, layer).start()

    own = pl.ds(width, pixels)

    def live_at(start, count):
        return info_ref[pl.ds(start, count), 0:1]

    def drop_chunk(chunk):
        load_bits(chunk).wait()
        start = pl.multiple_of(chunk * width, 16)
        target = cot[chunk].astype(f32) * live_at(width + start, width)
        task = lax.broadcasted_iota(jnp.int32, target.shape, 1) // HEAD_OUT
        parts = [jnp.where(task == k, target, 0.0).astype(bf16) for k in range(TASKS)]

        @pl.loop(0, channels // TILE)
        def _(tile):
            cols = pl.ds(pl.multiple_of(tile * TILE, TILE), TILE)
            table = hwt_ref[:, cols]
            signed = magnitude = weighted = None
            for part in parts:
                value = jnp.dot(part, table, preferred_element_type=f32)
                square = value * value
                whole = square + SOFT * SOFT
                inverse = lax.rsqrt(whole)
                if signed is None:
                    signed, magnitude, weighted = value, whole * inverse, square * inverse
                else:
                    signed = signed + value
                    magnitude = magnitude + whole * inverse
                    weighted = weighted + square * inverse
            level = bits[chunk % 2, :, cols].astype(f32)
            reach = 0.25 / SHARP
            inside = reach * (signed / magnitude) + (
                reach * (1.0 - 1.0 / LEVELS) - (2.0 * reach / LEVELS) * level
            )
            value = 0.5 * signed + (0.5 * jnp.tanh(inside)) * weighted
            merged[pl.ds(start, width), cols] = value.astype(bf16)

        if chunk + 2 < rows:
            load_bits(chunk + 2).start()

    live_all = info_ref[own, 0:1]
    count_here = jnp.sum(live_all, axis=0, keepdims=True)
    share = 1.0 / count_here

    def column_stats(values):
        mean = jnp.sum(values * live_all, axis=0, keepdims=True) * share
        apart = values - mean
        return mean, jnp.sum(live_all * apart * apart, axis=0, keepdims=True)

    def counts(step):
        return first_msg[step, 2:3, 0:1]

    def combine(slots):
        number = counts(0)
        mean = slots[0, 0:1] * counts(0)
        spread = slots[0, 1:2]
        for step in range(1, size):
            number = number + counts(step)
            mean = mean + slots[step, 0:1] * counts(step)
            spread = spread + slots[step, 1:2]
        mean = mean / number
        for step in range(size):
            apart = slots[step, 0:1] - mean
            spread = spread + counts(step) * apart * apart
        return mean, lax.rsqrt(spread / number + EPS), number

    load_u.wait()
    load_cot.wait()
    drop_chunk(0)
    first_msg[0, 2:3] = jnp.broadcast_to(count_here, (1, inner))
    first_msg[0, 3:4] = jnp.zeros((1, inner), f32)
    zc_out = za_out = zb_out = r1_out = None
    u1_out = pltpu.make_async_copy(u1, u1_hbm, out_sem.at[0])
    for layer in range(2):
        x_ref = (u0, u1)[layer]
        need_weight(0, layer)
        slots = first_msg if layer == 0 else msg.at[0]

        @pl.loop(0, inner // 256)
        def _(tile):
            cols = pl.ds(pl.multiple_of(tile * 256, 256), 256)
            values = jnp.dot(x_ref[...], wr[layer, :, cols], preferred_element_type=f32)
            a_ref[:, cols] = values
            mean, spread = column_stats(values)
            slots[0, 0:1, cols] = mean
            slots[0, 1:2, cols] = spread

        if layer == 1:
            for copy in (za_out, zb_out, r1_out, zc_out):
                copy.wait()
            u1_out.start()
        sends = link.copies(3 * layer, slots)
        for copy in sends:
            copy.start()
        a_edges = (a_ref.at[pl.ds(0, width)], a_ref.at[pl.ds(pixels - width, width)])
        a_halo = halo.at[2 * layer]
        link.start_edges(2 * layer, *a_edges, a_halo)
        if layer == 0:
            for kind in range(4):
                pushed_vector(kind).wait()
        drop_chunk(1 + 3 * layer)
        for copy in sends:
            copy.wait()
        mean, inverse, number = combine(slots)
        stat[layer, 0:1], stat[layer, 1:2] = mean, inverse
        rs_ref[layer, 0:1] = inverse
        rs_ref[layer, 2:3] = jnp.broadcast_to(number, (1, inner))
        link.wait_edges(2 * layer, *a_edges, a_halo)

        def first_act(row, values, inside):
            normed = (values - stat[layer, 0:1]) * stat[layer, 1:2]
            affine = normed * igs[layer, 0:1] + ibs[layer, 0:1]
            act = affine * (1.0 / (1.0 + jnp.exp(-affine)))
            if inside is not None:
                act = jnp.where(inside, act, 0.0)
            here = pl.ds(pl.multiple_of(row * width, 16), width)
            masks = info_ref[pl.ds(width, width), :]
            cat[here, 0:inner] = (pltpu.roll(act, 1, 0) * masks[:, 1:2]).astype(bf16)
            cat[here, inner : 2 * inner] = act.astype(bf16)
            cat[here, 2 * inner : 3 * inner] = (
                pltpu.roll(act, width - 1, 0) * masks[:, 2:3]
            ).astype(bf16)
            return normed

        first_act(0, a_halo[0], me > 0)
        first_act(rows + 1, a_halo[1], me < size - 1)

        @pl.loop(0, rows)
        def _(row):
            here = pl.ds(pl.multiple_of(row * width, 16), width)
            za[here] = first_act(row + 1, a_ref[here], None).astype(bf16)

        za_out = pltpu.make_async_copy(za, za_hbm.at[layer], out_sem.at[1])
        r1_out = pltpu.make_async_copy(
            cat.at[:, pl.ds(inner, inner)], r1_hbm.at[layer], out_sem.at[2]
        )
        za_out.start()
        r1_out.start()
        need_weight(1, layer)
        slots = msg.at[1 + 2 * layer]

        @pl.loop(0, inner // 256)
        def _(tile):
            cols = pl.ds(pl.multiple_of(tile * 256, 256), 256)
            values = None
            for tap in range(3):
                table = ws[layer, 3 * tap : 3 * tap + 3, :, cols].reshape(3 * inner, 256)
                value = jnp.dot(
                    cat[tap * width : tap * width + pixels], table, preferred_element_type=f32
                )
                values = value if values is None else values + value
            b_ref[:, cols] = values
            mean, spread = column_stats(values)
            slots[0, 0:1, cols] = mean
            slots[0, 1:2, cols] = spread

        sends = link.copies(3 * layer + 1, slots)
        for copy in sends:
            copy.start()
        b_edges = (b_ref.at[pl.ds(0, width)], b_ref.at[pl.ds(pixels - width, width)])
        b_halo = halo.at[2 * layer + 1]
        link.start_edges(2 * layer + 1, *b_edges, b_halo)
        drop_chunk(2 + 3 * layer)
        for copy in sends:
            copy.wait()
        mean, inverse, _ = combine(slots)
        stat[layer, 2:3], stat[layer, 3:4] = mean, inverse
        rs_ref[layer, 1:2] = inverse

        @pl.loop(0, rows)
        def _(row):
            here = pl.ds(pl.multiple_of(row * width, 16), width)
            normed = (b_ref[here] - stat[layer, 2:3]) * stat[layer, 3:4]
            zb[pl.ds(pl.multiple_of((row + 1) * width, 16), width)] = normed.astype(bf16)
            affine = normed * igs[layer, 1:2] + ibs[layer, 1:2]
            r2[here] = (affine * (1.0 / (1.0 + jnp.exp(-affine)))).astype(bf16)

        need_weight(2, layer)
        slots = msg_c.at[layer]

        @pl.loop(0, channels // 256)
        def _(tile):
            cols = pl.ds(pl.multiple_of(tile * 256, 256), 256)
            values = jnp.dot(r2[...], we[layer, :, cols], preferred_element_type=f32)
            e_ref[:, cols] = values
            mean, spread = column_stats(values)
            slots[0, 0:1, cols] = mean
            slots[0, 1:2, cols] = spread

        sends = link.copies(3 * layer + 2, slots)
        for copy in sends:
            copy.start()
        link.wait_edges(2 * layer + 1, *b_edges, b_halo)
        for side, row in ((0, 0), (1, rows + 1)):
            normed = (b_halo[side] - stat[layer, 2:3]) * stat[layer, 3:4]
            zb[row * width : (row + 1) * width] = normed.astype(bf16)
        zb_out = pltpu.make_async_copy(zb, zb_hbm.at[layer], out_sem.at[3])
        zb_out.start()
        drop_chunk(3 + 3 * layer)
        if layer == 1:
            drop_chunk(7)
            pltpu.make_async_copy(merged, merged_hbm, out_sem.at[4]).start()
        for copy in sends:
            copy.wait()
        mean, inverse, _ = combine(slots)
        stat_c[0:1], stat_c[1:2] = mean, inverse
        rc_ref[layer] = inverse
        out_ref = (u1, u0)[layer]

        @pl.loop(0, rows * (channels // TILE))
        def _(chunk):
            row, tile = chunk // (channels // TILE), chunk % (channels // TILE)
            here = pl.ds(pl.multiple_of(row * width, 16), width)
            cols = pl.ds(pl.multiple_of(tile * TILE, TILE), TILE)
            normed = (e_ref[here, cols] - stat_c[0:1, cols]) * stat_c[1:2, cols]
            zc[here, cols] = normed.astype(bf16)
            total = normed * ogs[layer, :, cols] + obs[layer, :, cols] + x_ref[here, cols].astype(f32)
            out_ref[here, cols] = (total * (1.0 / (1.0 + jnp.exp(-total)))).astype(bf16)

        zc_out = pltpu.make_async_copy(zc, zc_hbm.at[layer], out_sem.at[5])
        zc_out.start()

    heads_ref[...] = (
        lax.dot_general(u0[...], hwt_ref[...], BESIDE, preferred_element_type=f32) + hb_ref[...]
    )
    target = cot[...].astype(f32).reshape(pixels, -1) * live_all
    hbg_ref[...] = jnp.sum(target, axis=0, keepdims=True)
    target = target.astype(bf16)

    @pl.loop(0, channels // 256)
    def _(tile):
        cols = pl.ds(pl.multiple_of(tile * 256, 256), 256)
        hwg_ref[:, cols] = lax.dot_general(target, u0[:, cols], ACROSS, preferred_element_type=f32)

    for copy in (za_out, zb_out, r1_out, zc_out, u1_out):
        copy.wait()
    pltpu.make_async_copy(merged, merged_hbm, out_sem.at[4]).wait()
    for kind in range(3):
        pushed(kind).wait_send()
        for layer in range(2):
            save_weight(kind, layer).wait()


def forward(u, bits, cot, wr, ws, we, ig, ib, og, ob, hwt, hb, info):
    size = lax.axis_size("dp")
    pixels, channels = u.shape
    inner = wr.shape[1]
    _, rows, width, head_cols = cot.shape
    f32, bf16 = jnp.float32, jnp.bfloat16
    padded = pixels + 2 * width
    anywhere = pl.BlockSpec(memory_space=pl.ANY)
    vmem = pl.BlockSpec(memory_space=pltpu.VMEM)

    def out(kind, *shape):
        return jax.ShapeDtypeStruct(shape, kind)

    return pl.pallas_call(
        functools.partial(forward_kernel, size),
        out_shape=[
            out(f32, pixels, head_cols),
            out(f32, head_cols, channels),
            out(f32, 1, head_cols),
            out(f32, 2, 2, inner),
            out(f32, 2, 2, inner),
            out(f32, 2, 1, channels),
            out(f32, 2, 1, channels),
            out(f32, 2, 8, inner),
            out(f32, 2, 1, channels),
            out(bf16, pixels, channels),
            out(bf16, pixels, channels),
            out(bf16, 2, pixels, channels),
            out(bf16, 2, pixels, inner),
            out(bf16, 2, padded, inner),
            out(bf16, 2, padded, inner),
            out(bf16, 2, channels, inner),
            out(bf16, 2, 9, inner, inner),
            out(bf16, 2, inner, channels),
        ],
        in_specs=[anywhere] * 6 + [vmem] * 7,
        out_specs=[vmem] * 9 + [anywhere] * 9,
        scratch_shapes=[
            pltpu.VMEM((2, channels, inner), bf16),
            pltpu.VMEM((2, 9, inner, inner), bf16),
            pltpu.VMEM((2, inner, channels), bf16),
            pltpu.VMEM((pixels, channels), bf16),
            pltpu.VMEM((pixels, channels), bf16),
            pltpu.VMEM((pixels, inner), f32),
            pltpu.VMEM((pixels, inner), f32),
            pltpu.VMEM((pixels, channels), f32),
            pltpu.VMEM((padded, 3 * inner), bf16),
            pltpu.VMEM((pixels, inner), bf16),
            pltpu.VMEM((pixels, inner), bf16),
            pltpu.VMEM((padded, inner), bf16),
            pltpu.VMEM((pixels, channels), bf16),
            pltpu.VMEM((pixels, channels), bf16),
            pltpu.VMEM((2, width, channels), jnp.int32),
            pltpu.VMEM((rows, width, head_cols), bf16),
            pltpu.VMEM((4, 2, width, inner), f32),
            pltpu.VMEM((4, size, 2, inner), f32),
            pltpu.VMEM((2, size, 2, channels), f32),
            pltpu.VMEM((size, 4, inner), f32),
            pltpu.VMEM((2, 8, inner), f32),
            pltpu.VMEM((2, channels), f32),
            pltpu.SemaphoreType.DMA((6, size)),
            pltpu.SemaphoreType.DMA((6, size)),
            pltpu.SemaphoreType.DMA((4, 2)),
            pltpu.SemaphoreType.DMA((4, 2)),
            pltpu.SemaphoreType.DMA((3,)),
            pltpu.SemaphoreType.DMA((7,)),
            pltpu.SemaphoreType.DMA((7,)),
            pltpu.SemaphoreType.DMA((3, 2)),
            pltpu.SemaphoreType.DMA((2,)),
            pltpu.SemaphoreType.DMA((2,)),
            pltpu.SemaphoreType.DMA((6,)),
        ],
        compiler_params=pltpu.CompilerParams(
            collective_id=1, has_side_effects=True, vmem_limit_bytes=LIMIT
        ),
    )(u, bits, cot, wr, ws, we, ig, ib, og, ob, hwt, hb, info)


def backward_kernel(
    size,
    u0_hbm,
    u1_hbm,
    merged_hbm,
    zc_hbm,
    za_hbm,
    zb_hbm,
    r1_hbm,
    wr_all,
    ws_all,
    we_all,
    igs,
    ibs,
    ogs,
    obs,
    rs_ref,
    rc_ref,
    hwg_ref,
    hbg_ref,
    info_ref,
    grad_hbm,
    parts,
    wr,
    ws,
    we,
    u_ref,
    d_ref,
    de,
    zc,
    za,
    zb,
    r1,
    r2,
    cat,
    dzb,
    dza,
    da,
    stage,
    small,
    halo,
    msg,
    msg_c,
    part_sum,
    sums,
    sums_c,
    send_sem,
    recv_sem,
    edge_send,
    edge_recv,
    in_sem,
    tile_sem,
    out_sem,
):
    link = Exchange(size, send_sem, recv_sem, edge_send, edge_recv)
    section, me = link.section, link.me
    pixels, channels = d_ref.shape
    inner = da.shape[1]
    width = halo.shape[2]
    rows = pixels // width
    across = channels // TILE
    f32, bf16 = jnp.float32, jnp.bfloat16
    own = pl.ds(width, pixels)

    def loads(layer):
        return {
            "zc": pltpu.make_async_copy(zc_hbm.at[layer], zc, in_sem.at[0]),
            "za": pltpu.make_async_copy(za_hbm.at[layer], za, in_sem.at[1]),
            "zb": pltpu.make_async_copy(zb_hbm.at[layer], zb, in_sem.at[2]),
            "r1": pltpu.make_async_copy(r1_hbm.at[layer], r1, in_sem.at[3]),
            "wr": pltpu.make_async_copy(wr_all.at[layer], wr, in_sem.at[4]),
            "ws": pltpu.make_async_copy(ws_all.at[layer], ws, in_sem.at[5]),
            "we": pltpu.make_async_copy(we_all.at[layer], we, in_sem.at[6]),
            "u": pltpu.make_async_copy((u0_hbm, u1_hbm)[layer], u_ref.at[layer], in_sem.at[7 + layer]),
        }

    load_d = pltpu.make_async_copy(merged_hbm, d_ref, in_sem.at[9])
    first, second = loads(1), loads(0)
    load_d.start()
    for name in ("u", "zc", "we", "zb", "ws", "za", "r1", "wr"):
        first[name].start()
    second["u"].start()
    link.greet()
    live_all = info_ref[own, 0:1]

    def stage_copy(slot, tile):
        return pltpu.make_async_copy(stage.at[slot], parts.at[tile], tile_sem.at[slot])

    def put_tile(base, index, make):
        slot = lax.rem(index, 2)
        pl.when(base + index >= 2)(lambda: stage_copy(slot, 0).wait())

        @pl.loop(0, 2)
        def _(side):
            cols = pl.ds(pl.multiple_of(side * 256, 256), 256)
            stage[slot, :, cols] = make(side).astype(bf16)

        stage_copy(slot, base + index).start()

    def column_sums(values):
        return jnp.sum(values, axis=0, keepdims=True)

    def total_of(slots):
        found = slots[0]
        for step in range(1, size):
            found = found + slots[step]
        return found

    def expand_tiles(base):
        @pl.loop(0, across)
        def _(tile):
            def make(side):
                cols = pl.ds(pl.multiple_of(tile * TILE + side * 256, 256), 256)
                return lax.dot_general(r2[...], de[:, cols], ACROSS, preferred_element_type=f32)

            put_tile(base, tile, make)

    def spatial_tiles(base):
        @pl.loop(0, 9)
        def _(tap):
            shift, side_step = tap // 3, tap % 3

            def make(side):
                at = pl.ds(pl.multiple_of(shift * width, 16), pixels)
                cols = pl.ds(pl.multiple_of(side_step * inner + side * 256, 256), 256)
                return lax.dot_general(r1[at], cat[own, cols], ACROSS, preferred_element_type=f32)

            put_tile(base, across + tap, make)

    def reduce_tiles_of(base, layer):
        @pl.loop(0, across)
        def _(tile):
            def make(side):
                cols = pl.ds(pl.multiple_of(side * 256, 256), 256)
                lines = pl.ds(pl.multiple_of(tile * TILE, TILE), TILE)
                return lax.dot_general(
                    u_ref[layer, :, lines], da[:, cols], ACROSS, preferred_element_type=f32
                )

            put_tile(base, across + 9 + tile, make)

    def small_tile(base, layer):
        last = 2 * across + 9
        half = channels // 2
        head_cols = hwg_ref.shape[0]
        slot = last % 2
        stage_copy(slot, 0).wait()
        small[...] = jnp.zeros_like(small)
        for k in range(2):
            at = layer * half + k * TILE
            small[k * head_cols : (k + 1) * head_cols] = hwg_ref[:, at : at + TILE]
        row = 2 * head_cols
        small[row : row + 1, 0:head_cols] = hbg_ref[...]
        only = (me == 0).astype(f32)
        small[row + 8 : row + 9] = sums[0, 1:2] * only
        small[row + 9 : row + 10] = sums[1, 1:2] * only
        small[row + 10 : row + 11] = sums[0, 0:1] * only
        small[row + 11 : row + 12] = sums[1, 0:1] * only
        for k in range(across):
            cols = slice(k * TILE, (k + 1) * TILE)
            small[row + 12 + k : row + 13 + k] = sums_c[1:2, cols] * only
            small[row + 12 + across + k : row + 13 + across + k] = sums_c[0:1, cols] * only
        stage[slot] = jnp.zeros_like(stage[slot])
        stage[slot, 0 : small.shape[0]] = small[...].astype(bf16)
        stage_copy(slot, base + last).start()

    load_d.wait()
    for layer in (1, 0):
        base = (1 - layer) * (2 * across + 10)
        now = (second, first)[layer]
        now["u"].wait()
        now["zc"].wait()
        part_sum[...] = jnp.zeros_like(part_sum)

        @pl.loop(0, rows * across)
        def _(chunk):
            row, tile = chunk // across, chunk % across
            here = pl.ds(pl.multiple_of(row * width, 16), width)
            cols = pl.ds(pl.multiple_of(tile * TILE, TILE), TILE)
            normed = zc[here, cols].astype(f32)
            total = (
                normed * ogs[layer, :, cols]
                + obs[layer, :, cols]
                + u_ref[layer, here, cols].astype(f32)
            )
            _, slope = silu_parts(total)
            dt = d_ref[here, cols].astype(f32) * slope
            d_ref[here, cols] = dt.astype(bf16)
            part_sum[0, :, cols] += folded(dt)
            part_sum[1, :, cols] += folded(dt * normed)

        slots = msg_c.at[1 - layer]
        slots[0, 0:1] = column_sums(part_sum[0])
        slots[0, 1:2] = column_sums(part_sum[1])
        sends = link.copies(3 * layer, slots)
        for copy in sends:
            copy.start()
        if layer == 0:
            reduce_tiles_of(0, 1)
            small_tile(0, 1)
        for copy in sends:
            copy.wait()
        sums_c[...] = total_of(slots)
        number = rs_ref[layer, 2:3, 0:1]
        share = 1.0 / number

        @pl.loop(0, rows * across)
        def _(chunk):
            row, tile = chunk // across, chunk % across
            here = pl.ds(pl.multiple_of(row * width, 16), width)
            cols = pl.ds(pl.multiple_of(tile * TILE, TILE), TILE)
            live = info_ref[pl.ds(pl.multiple_of((row + 1) * width, 16), width), 0:1]
            normed = zc[here, cols].astype(f32)
            away = (sums_c[0:1, cols] + normed * sums_c[1:2, cols]) * share
            scale = rc_ref[layer, :, cols] * ogs[layer, :, cols]
            value = scale * (d_ref[here, cols].astype(f32) - live * away)
            de[here, cols] = value.astype(bf16)

        now["we"].wait()
        now["zb"].wait()
        slots = msg.at[2 * layer]

        @pl.loop(0, inner // 256)
        def _(tile):
            cols = pl.ds(pl.multiple_of(tile * 256, 256), 256)
            dr2 = lax.dot_general(de[...], we[cols], BESIDE, preferred_element_type=f32)
            normed = zb[own, cols].astype(f32)
            act, slope = silu_parts(normed * igs[layer, 1:2, cols] + ibs[layer, 1:2, cols])
            r2[:, cols] = act.astype(bf16)
            dz = dr2 * slope
            dzb[:, cols] = dz
            slots[0, 0:1, cols] = column_sums(dz)
            slots[0, 1:2, cols] = column_sums(dz * normed)

        sends = link.copies(3 * layer + 1, slots)
        for copy in sends:
            copy.start()
        edges = (dzb.at[pl.ds(0, width)], dzb.at[pl.ds(pixels - width, width)])
        landing = halo.at[layer]
        link.start_edges(layer, *edges, landing)
        if layer == 1:
            second["zc"].start()
            second["we"].start()
        expand_tiles(base)
        for copy in sends:
            copy.wait()
        sums[1] = total_of(slots)
        link.wait_edges(layer, *edges, landing)

        def db_row(row, dz, inside):
            here = pl.ds(pl.multiple_of(row * width, 16), width)
            live = info_ref[here, 0:1]
            normed = zb[here].astype(f32)
            away = (sums[1, 0:1] + normed * sums[1, 1:2]) * share
            value = (rs_ref[layer, 1:2] * igs[layer, 1:2]) * (dz - live * away)
            if inside is not None:
                value = jnp.where(inside, value, 0.0)
            masks = info_ref[pl.ds(width, width), :]
            cat[here, 0:inner] = (pltpu.roll(value, width - 1, 0) * masks[:, 2:3]).astype(bf16)
            cat[here, inner : 2 * inner] = value.astype(bf16)
            cat[here, 2 * inner : 3 * inner] = (
                pltpu.roll(value, 1, 0) * masks[:, 1:2]
            ).astype(bf16)

        db_row(0, landing[0], me > 0)
        db_row(rows + 1, landing[1], me < size - 1)

        @pl.loop(0, rows)
        def _(row):
            db_row(row + 1, dzb[pl.ds(pl.multiple_of(row * width, 16), width)], None)

        if layer == 1:
            second["zb"].start()
        now["ws"].wait()
        now["za"].wait()
        slots = msg.at[2 * layer + 1]

        @pl.loop(0, inner // 256)
        def _(tile):
            cols = pl.ds(pl.multiple_of(tile * 256, 256), 256)
            dr1 = None
            for tap in range(9):
                start = (2 - tap // 3) * width
                block = cat[start : start + pixels, (tap % 3) * inner : (tap % 3 + 1) * inner]
                value = lax.dot_general(block, ws[tap, cols], BESIDE, preferred_element_type=f32)
                dr1 = value if dr1 is None else dr1 + value
            normed = za[:, cols].astype(f32)
            _, slope = silu_parts(normed * igs[layer, 0:1, cols] + ibs[layer, 0:1, cols])
            dz = dr1 * slope
            dza[:, cols] = dz
            slots[0, 0:1, cols] = column_sums(dz)
            slots[0, 1:2, cols] = column_sums(dz * normed)

        sends = link.copies(3 * layer + 2, slots)
        for copy in sends:
            copy.start()
        if layer == 1:
            second["ws"].start()
        now["r1"].wait()
        spatial_tiles(base)
        for copy in sends:
            copy.wait()
        sums[0] = total_of(slots)
        if layer == 1:
            second["r1"].start()

        @pl.loop(0, rows)
        def _(row):
            here = pl.ds(pl.multiple_of(row * width, 16), width)
            live = info_ref[pl.ds(pl.multiple_of((row + 1) * width, 16), width), 0:1]
            away = (sums[0, 0:1] + za[here].astype(f32) * sums[0, 1:2]) * share
            value = (rs_ref[layer, 0:1] * igs[layer, 0:1]) * (dza[here] - live * away)
            da[here] = value.astype(bf16)

        if layer == 1:
            second["za"].start()
        now["wr"].wait()

        @pl.loop(0, channels // 256)
        def _(tile):
            cols = pl.ds(pl.multiple_of(tile * 256, 256), 256)
            du = lax.dot_general(da[...], wr[cols], BESIDE, preferred_element_type=f32)
            d_ref[:, cols] = (du + d_ref[:, cols].astype(f32)).astype(bf16)

        if layer == 1:
            second["wr"].start()
    out = pltpu.make_async_copy(d_ref, grad_hbm, out_sem)
    out.start()
    reduce_tiles_of(2 * across + 10, 0)
    small_tile(2 * across + 10, 0)
    stage_copy(0, 0).wait()
    stage_copy(1, 0).wait()
    out.wait()


def backward(u0, u1, merged, zc, za, zb, r1, wr, ws, we, igs, ibs, ogs, obs, rs, rc, hwg, hbg, info):
    size = lax.axis_size("dp")
    pixels, channels = u0.shape
    inner = za.shape[2]
    padded = zb.shape[1]
    width = (padded - pixels) // 2
    f32, bf16 = jnp.float32, jnp.bfloat16
    anywhere = pl.BlockSpec(memory_space=pl.ANY)
    vmem = pl.BlockSpec(memory_space=pltpu.VMEM)
    count = 2 * (2 * (channels // TILE) + 10)
    return pl.pallas_call(
        functools.partial(backward_kernel, size),
        out_shape=[
            jax.ShapeDtypeStruct((pixels, channels), bf16),
            jax.ShapeDtypeStruct((count, TILE, TILE), bf16),
        ],
        in_specs=[anywhere] * 10 + [vmem] * 9,
        out_specs=[anywhere] * 2,
        scratch_shapes=[
            pltpu.VMEM((channels, inner), bf16),
            pltpu.VMEM((9, inner, inner), bf16),
            pltpu.VMEM((inner, channels), bf16),
            pltpu.VMEM((2, pixels, channels), bf16),
            pltpu.VMEM((pixels, channels), bf16),
            pltpu.VMEM((pixels, channels), bf16),
            pltpu.VMEM((pixels, channels), bf16),
            pltpu.VMEM((pixels, inner), bf16),
            pltpu.VMEM((padded, inner), bf16),
            pltpu.VMEM((padded, inner), bf16),
            pltpu.VMEM((pixels, inner), bf16),
            pltpu.VMEM((padded, 3 * inner), bf16),
            pltpu.VMEM((pixels, inner), f32),
            pltpu.VMEM((pixels, inner), f32),
            pltpu.VMEM((pixels, inner), bf16),
            pltpu.VMEM((2, TILE, TILE), bf16),
            pltpu.VMEM((128, TILE), f32),
            pltpu.VMEM((2, 2, width, inner), f32),
            pltpu.VMEM((4, size, 2, inner), f32),
            pltpu.VMEM((2, size, 2, channels), f32),
            pltpu.VMEM((2, 8, channels), f32),
            pltpu.VMEM((2, 2, inner), f32),
            pltpu.VMEM((2, channels), f32),
            pltpu.SemaphoreType.DMA((6, size)),
            pltpu.SemaphoreType.DMA((6, size)),
            pltpu.SemaphoreType.DMA((2, 2)),
            pltpu.SemaphoreType.DMA((2, 2)),
            pltpu.SemaphoreType.DMA((10,)),
            pltpu.SemaphoreType.DMA((2,)),
            pltpu.SemaphoreType.DMA,
        ],
        compiler_params=pltpu.CompilerParams(
            collective_id=2, has_side_effects=True, vmem_limit_bytes=LIMIT
        ),
    )(u0, u1, merged, zc, za, zb, r1, wr, ws, we, igs, ibs, ogs, obs, rs, rc, hwg, hbg, info)


def pixel_info(pixel_mask, starts):
    size = lax.axis_size("dp")
    rows, width = pixel_mask.shape
    up = [(i, i + 1) for i in range(size - 1)]
    down = [(j, i) for i, j in up]
    before = lax.ppermute(pixel_mask[rows - 1 :], "dp", up)
    after = lax.ppermute(pixel_mask[:1], "dp", down)
    live = jnp.concatenate([before, pixel_mask, after])
    columns = jnp.arange(width, dtype=jnp.int32)
    crop = jnp.sum((columns[:, None] >= starts[None, :]).astype(jnp.int32), axis=1)
    outside = jnp.full((1,), -1, jnp.int32)
    left = jnp.concatenate([outside, crop[:-1]]) == crop
    right = jnp.concatenate([crop[1:], outside]) == crop
    lane = jnp.arange(128, dtype=jnp.int32)
    first = jnp.where(lane == 0, live[:, :, None], 0)
    links = jnp.where(lane == 1, left[:, None].astype(jnp.int32), 0)
    links = links + jnp.where(lane == 2, right[:, None].astype(jnp.int32), 0)
    return (first + links[None]).astype(jnp.float32).reshape(-1, 128)


def pick(array, index):
    return lax.dynamic_index_in_dim(array, index, 0, keepdims=False)


def local(
    canvases,
    crop_starts,
    pixel_mask,
    drop_bits,
    reduce_weight,
    spatial_weight,
    expand_weight,
    inner_gain,
    inner_bias,
    outer_gain,
    outer_bias,
    head_weight,
    head_bias,
    head_cotangent,
):
    section = lax.axis_index("section")
    first = section == 0
    rows, width, channels = canvases.shape[1:]
    taps = spatial_weight.shape[1]
    head_cols = head_weight.shape[1]
    pixels = rows * width
    flat = canvases.reshape(pixels, channels)
    info = pixel_info(pick(pixel_mask, section), pick(crop_starts, section))
    heads, hwg, hbg, igs, ibs, ogs, obs, rs, rc, merged, u1, zc, za, zb, r1, wr, ws, we = forward(
        flat,
        drop_bits,
        head_cotangent,
        reduce_weight[0],
        spatial_weight[0],
        expand_weight[0],
        inner_gain[0],
        inner_bias[0],
        outer_gain,
        outer_bias,
        head_weight.T,
        head_bias[None],
        info,
    )
    grad, parts = backward(
        flat, u1, merged, zc, za, zb, r1, wr, ws, we, igs, ibs, ogs, obs, rs, rc, hwg, hbg, info
    )
    expand_total, spatial_total, reduce_total, small = reduce_tiles(parts, channels, taps)
    small = small.astype(jnp.float32)
    half = channels // 2
    across = channels // TILE
    head_w_out = jnp.concatenate([small[:head_cols].T, small[head_cols : 2 * head_cols].T])
    row = 2 * head_cols
    cut = head_cols // 2
    head_b_out = jnp.where(first, small[row, :cut], small[row, cut:head_cols])
    norms = small[row + 8 :]
    return (
        heads.reshape(1, rows, width, head_cols),
        grad.reshape(1, rows, width, channels),
        reduce_total.astype(jnp.float32)[None],
        spatial_total.astype(jnp.float32)[None],
        expand_total.astype(jnp.float32)[None],
        norms[0:2][None],
        norms[2:4][None],
        norms[4 : 4 + across].reshape(1, channels),
        norms[4 + across : 4 + 2 * across].reshape(1, channels),
        head_w_out,
        head_b_out,
    )


def solution(mesh):
    placed = (
        P("section", "dp", None, None),
        P(),
        P(None, "dp", None),
        P(None, "dp", None, None),
        P("section", None, None),
        P("section", None, None, None),
        P("section", None, None),
        P("section", None, None),
        P("section", None, None),
        P("section", None),
        P("section", None),
        P(),
        P(),
        P(None, "dp", None, None),
    )
    return jax.shard_map(
        local,
        mesh=mesh,
        in_specs=placed,
        out_specs=(
            P("section", "dp", None, None),
            P("section", "dp", None, None),
            P("section", None, None),
            P("section", None, None, None),
            P("section", None, None),
            P("section", None, None),
            P("section", None, None),
            P("section", None),
            P("section", None),
            P("section", None),
            P("section"),
        ),
        check_vma=False,
    )
```

time: 902 us -> 397 us (0.44); the launches traced: 892 us -> 396 us
  local copies, waits for them, and re-layouts: 280 us -> 10.2 us
  matrix products: 151 us -> 0 us
  other arithmetic: 122 us -> 17.5 us
  Pallas kernels: 307 us -> 360 us
  starting transfers between devices: 21.7 us -> 6.12 us
    dot_general x23 -> x0, matrix products: 151 us -> none  [the longest x3 31.4 us: heads_step(): lax.dot_general(target[:, start:start + HEAD_OUT], head_weight[:, start:s...]
    unnamed x270 -> x20, local copies, waits for them, and re-layouts: 86 us -> 7.02 us
    concatenate x39 -> x0, local copies, waits for them, and re-layouts: 53.4 us -> none  [the longest x36 52.4 us: patches(): return jnp.concatenate(blocks, axis=2).reshape(rows * width, -1)]
    pallas_call x12 -> x2, Pallas kernels: 138 us -> 190 us  [the longest x1 95.7 us: backward(): pl.pallas_call(functools.partial(backward_kernel, size), out_shape=[jax.S...]
    slice x30 -> x2, local copies, waits for them, and re-layouts: 47.8 us -> 0.08 us  [the longest x1 0.07 us: pixel_info(): left = jnp.concatenate([outside, crop[:-1]]) == crop]
    reshape x16 -> x0, local copies, waits for them, and re-layouts: 39.9 us -> none  [the longest x7 29.1 us: rows_first(): x = x.astype(jnp.bfloat16).reshape(-1, TILE, nx, cols)]
    convert_element_type x11 -> x3, other arithmetic: 41.9 us -> 3.35 us  [the longest x1 2.29 us: local(): small = small.astype(jnp.float32)]
    convert_element_type x8 -> x0, local copies, waits for them, and re-layouts: 28.2 us -> none  [the longest x1 18.7 us: local(): jnp.swapaxes(total, 1, 2).reshape(-1, TILE, TILE).astype(jnp.float32)]
  transfers between devices with their start and end apart: 15 -> 2, of which waited for: 2 -> 1; matrix products, arithmetic and copies ran while one was open for 17% -> 1% of each run, Pallas kernels for 4% -> 0%
where the time goes in v2:
time: 397 us; the launch traced here: 396 us
  Pallas kernels  360 us (91%)
  other arithmetic  17.5 us (4%)
  local copies, waits for them, and re-layouts  10.2 us (3%)
  starting transfers between devices  6.12 us (2%)
    pallas_call x1, Pallas kernels, reduce_tiles(): pl.pallas_call(functools.partial(reduce_kernel, size, groups), out_shape=...  171 us
    pallas_call x1, Pallas kernels, backward(): pl.pallas_call(functools.partial(backward_kernel, size), out_shape=[jax.S...  95.7 us
    pallas_call x1, Pallas kernels, forward(): pl.pallas_call(functools.partial(forward_kernel, size), out_shape=[out(f3...  93.8 us
  transfers between devices with their start and end apart: 2, of which 1 were waited for; matrix products, arithmetic and copies ran while one was open for 1% of the time, Pallas kernels for 0%

profile of v2, /device:TPU:0, one launch (start us, length us, event | category | flops | bytes accessed | tf_op | source)
XLA Modules:
  0.0 396.2 jit_solution(11118885630173798209)
XLA Ops:
  0.7 0.7 copy-done
  1.4 4.8 %collective-permute-start = (s32[1,96]{1,0:T(1,128)S(1)}, s32[1,96]{1,0:T(1,128)S(1)}, u32[]{:S(2)}, u32[]{:S(2)}) collective-permute-start(s32[1,96]{1,0:T(1,128)S(1)} %get-tuple-element.87), channel_id=1, source_target_pairs={{0,1},{1,2},{2,3},{3,4},{4,5},{5,6},{6,7},{7,8},{8,9},{9,10},{10,1... | collective-permute-start | bytes 1160 | tf_op jit(solution)/shard_map/ppermute | solution.py:1271
  6.2 1.3 collective-permute-start.1
  7.5 0.7 dynamic-slice_bitcast_fusion
  8.5 0.1 select_add_fusion
  8.6 1.9 copy.27.cot_hbm
  10.4 1.2 collective-permute-done.1
  11.7 1.0 fusion.info_ref
  12.7 93.8 %shard_map.221 = (f32[768,48]{1,0:T(8,128)}, f32[48,2048]{1,0:T(8,128)}, f32[1,48]{1,0:T(1,128)}, f32[2,2,512]{2,1,0:T(2,128)}, f32[2,2,512]{2,1,0:T(2,128)}, /*...) custom-call(bf16[768,2048]{1,0:T(8,128)(2,1)} %bitcast.49, ...), custom_call_target="tpu_custom_call" | custom-call | tf_op jit(solution)/shard_map/pallas_call | solution.py:810
  106.5 95.7 %shard_map.222 = (bf16[768,2048]{1,0:T(8,128)(2,1)}, bf16[36,512,512]{2,1,0:T(8,128)(2,1)}) custom-call(bf16[768,2048]{1,0:T(8,128)(2,1)} %bitcast.50, bf16[768,2048]{1,0:T(8,128)(2,1)} %get-tuple-element.36.u1_hbm, bf16[768,2048]{1,0:T(8,128)(2,1)} %get-tuple-element.37.merged_hbm, bf16[2,768,2048]{2,1,0:T(8,128)(2,1)} %get-tuple-element.38.zc_hbm, ...), custom_call_target="tpu_custom_call" | custom-call | tf_op jit(solution)/shard_map/pallas_call | solution.py:1220
  202.2 170.8 %shard_map.223 = (bf16[512,2048]{1,0:T(8,128)(2,1)}, bf16[9,512,512]{2,1,0:T(8,128)(2,1)}, bf16[2048,512]{1,0:T(8,128)(2,1)}, bf16[512,512]{1,0:T(8,128)(2,1)}) custom-call(bf16[36,512,512]{2,1,0:T(8,128)(2,1)} %get-tuple-element.54.parts), custom_call_target="tpu_custom_call" | custom-call | tf_op jit(solution)/shard_map/pallas_call | solution.py:341
  373.0 2.3 convert_element_type.33
  375.3 1.4 slice_bitcast_fusion.4
  376.7 0.7 slice_bitcast_fusion.2
  377.5 1.0 slice_bitcast_fusion.1
  378.5 0.8 copy.28
  379.3 1.3 fusion.1
  380.6 0.6 copy.30
  381.2 0.6 copy.29
  381.8 4.3 %bitcast_convert_fusion.2 = f32[1,2048,512]{2,1,0:T(8,128)} fusion(bf16[2048,512]{1,0:T(8,128)(2,1)} %get-tuple-element.55), kind=kLoop, calls=%fused_computation.2 | loop fusion | flops 1048576 | bytes 6291456 | tf_op jit(solution)/shard_map/broadcast_in_dim | solution.py:1344
  386.2 2.5 bitcast_convert_fusion.1
  388.8 5.1 %bitcast_convert_fusion = f32[1,9,512,512]{3,2,1,0:T(8,128)} fusion(bf16[9,512,512]{2,1,0:T(8,128)(2,1)S(1)} %bitcast.52), kind=kLoop, calls=%fused_computation | loop fusion | flops 2359296 | bytes 14155776 | tf_op jit(solution)/shard_map/broadcast_in_dim | solution.py:1345
  393.8 0.7 pad_maximum_fusion
  394.5 1.7 copy.32
  (25 shorter events, 0.4 us)
Async XLA Ops:
  0.6 0.7 copy-start
  1.4 9.1 %collective-permute-start = (s32[1,96]{1,0:T(1,128)S(1)}, s32[1,96]{1,0:T(1,128)S(1)}, u32[]{:S(2)}, u32[]{:S(2)}) collective-permute-start(s32[1,96]{1,0:T(1,128)S(1)} %get-tuple-element.87), channel_id=1, source_target_pairs={{0,1},{1,2},{2,3},{3,4},{4,5},{5,6},{6,7},{7,8},{8,9},{9,10},{10,1... | collective-permute-start | bytes 1160 | tf_op jit(solution)/shard_map/ppermute | solution.py:1271
  6.2 5.4 %collective-permute-start.1 = (s32[1,96]{1,0:T(1,128)S(1)}, s32[1,96]{1,0:T(1,128)S(1)}, u32[]{:S(2)}, u32[]{:S(2)}) collective-permute-start(s32[1,96]{1,0:T(1,128)S(1)} %get-tuple-element.88), channel_id=1, source_target_pairs={{1,0},{2,1},{3,2},{4,3},{5,4},{6,5},{7,6},{8,7},{9,8},{10,9},{11,1... | collective-permute-start | bytes 1160 | tf_op jit(solution)/shard_map/ppermute | solution.py:1272
  202.2 176.2 %copy-start.4 = (f32[768,48]{1,0:T(8,128)S(1)}, f32[768,48]{1,0:T(8,128)}, u32[]{:S(2)}) copy-start(f32[768,48]{1,0:T(8,128)} %get-tuple-element.35) | copy-start | bytes 442372
  373.0 13.2 %copy-start.3 = (bf16[512,2048]{1,0:T(8,128)(2,1)S(1)}, bf16[512,2048]{1,0:T(8,128)(2,1)}, u32[]{:S(2)}) copy-start(bf16[512,2048]{1,0:T(8,128)(2,1)} %get-tuple-element.57) | copy-start | bytes 6291460
  378.4 10.3 %slice-start = ((s8[4718592]{0:T(1024)(128)(4,1)}), s8[524288]{0:T(1024)(128)(4,1)S(1)}, s32[]{:S(2)}) async-start(s8[4718592]{0:T(1024)(128)(4,1)} %bitcast.51), calls=%async_computation | async-start | bytes 1048576
  381.8 6.9 %slice-start.1 = ((s8[4718592]{0:T(1024)(128)(4,1)}), s8[4194304]{0:T(1024)(128)(4,1)S(1)}, s32[]{:S(2)}) async-start(s8[4718592]{0:T(1024)(128)(4,1)} %bitcast.51), calls=%async_computation.1 | async-start | bytes 8388608
  388.7 5.8 %copy-start.2 = (bf16[768,2048]{1,0:T(8,128)(2,1)S(1)}, bf16[768,2048]{1,0:T(8,128)(2,1)}, u32[]{:S(2)}) copy-start(bf16[768,2048]{1,0:T(8,128)(2,1)} %get-tuple-element.53) | copy-start | bytes 9437188
  388.8 7.4 %copy-start.1 = (s32[2,8,96]{2,1,0:T(8,128)S(1)}, s32[2,8,96]{2,1,0:T(8,128)}, u32[]{:S(2)}) copy-start(s32[2,8,96]{2,1,0:T(8,128)} %param.16) | copy-start | bytes 18436

commit v3 on v2

--- a/solution.py
+++ b/solution.py
@@ -30,23 +30,27 @@
 
 class Reducer:
     STAGES = 9
-    RING = 4
-
-    def __init__(self, size, groups):
+
+    def __init__(self, size, tiles):
         self.size = size
-        self.groups = groups
         self.nz, self.ny, self.nx = grid_of(size)
-        self.half = TILE // 2
+        self.zrows = 16
+        self.yrows = self.zrows * self.nz
+        self.half = self.yrows * self.ny
+        self.lines = 2 * self.half
         self.cols = TILE // self.nx
-        self.yrows = self.half // self.ny
-        self.zrows = self.yrows // self.nz
+        self.per_tile = TILE // self.lines
+        self.lag = 2 if self.per_tile > 1 else 1
+        self.slots = 4 * self.lag + 2
+        self.real = tiles * self.per_tile + 1
+        self.block_groups = -(-self.real // 3)
+        self.groups = 2 * self.block_groups
 
     def scratch(self):
         nx, ny, nz, groups, cols = self.nx, self.ny, self.nz, self.groups, self.cols
         bf16 = jnp.bfloat16
         return [
-            pltpu.VMEM((3 * self.RING, self.half, TILE), bf16),
-            pltpu.VMEM((3 * groups, self.half, TILE), bf16),
+            pltpu.VMEM((3 * self.slots, self.lines, TILE), bf16),
             pltpu.VMEM((3 * groups, self.half, TILE), bf16),
             pltpu.VMEM((2 * groups, nx - 1, self.half, cols), bf16),
             pltpu.VMEM((2 * groups, ny - 1, self.yrows, cols), bf16),
@@ -60,12 +64,11 @@
             pltpu.SemaphoreType.DMA((3 * groups, 2 * (nx + ny + nz - 3))),
         ]
 
-    def bind(self, parts, total, scratch):
-        self.parts, self.total = parts, total
+    def bind(self, total, scratch):
+        self.total = total
         (
             self.ring,
             self.res,
-            self.sec,
             self.ax,
             self.ay,
             self.az,
@@ -83,20 +86,6 @@
         self.y = (self.me // self.nx) % self.ny
         self.x = self.me % self.nx
 
-    def peers(self):
-        found = [(1 - self.section, self.me)]
-        for axis in "xyz":
-            for step in range(1, self.count(axis)):
-                found.append((self.section, self.other(axis, step)[0]))
-        return found
-
-    def greet(self):
-        barrier = pltpu.get_barrier_semaphore()
-        peers = self.peers()
-        for peer in peers:
-            pl.semaphore_signal(barrier, inc=1, device_id=peer, device_id_type=MESH)
-        pl.semaphore_wait(barrier, len(peers))
-
     def count(self, axis):
         return {"x": self.nx, "y": self.ny, "z": self.nz}[axis]
 
@@ -115,8 +104,11 @@
         base = {"x": 0, "y": self.nx - 1, "z": self.nx + self.ny - 2}[axis]
         return base + (step - 1) + (self.nx + self.ny + self.nz - 3 if back else 0)
 
-    def acc(self, tile):
-        return self.ring.at[lax.rem(tile, 3 * self.RING)]
+    def slot(self, unit):
+        return self.ring.at[lax.rem(unit, 3 * self.slots)]
+
+    def acc(self, unit):
+        return self.slot(unit).at[self.half_rows(self.section)]
 
     def block(self, base, x, y, z):
         if y is None:
@@ -176,21 +168,15 @@
     def half_rows(self, which):
         return pl.ds(pl.multiple_of(which * self.half, 16), self.half)
 
-    def pair(self, tile):
-        own = pltpu.make_async_copy(
-            self.parts.at[tile, self.half_rows(self.section)],
-            self.acc(tile),
-            self.pair_send.at[tile, 0],
-        )
-        away = pltpu.make_async_remote_copy(
-            src_ref=self.parts.at[tile, self.half_rows(1 - self.section)],
-            dst_ref=self.sec.at[tile],
-            send_sem=self.pair_send.at[tile, 1],
-            recv_sem=self.pair_recv.at[tile, 0],
+    def pair(self, unit):
+        return pltpu.make_async_remote_copy(
+            src_ref=self.slot(unit).at[self.half_rows(1 - self.section)],
+            dst_ref=self.res.at[unit],
+            send_sem=self.pair_send.at[unit, 1],
+            recv_sem=self.pair_recv.at[unit, 0],
             device_id=(1 - self.section, self.me),
             device_id_type=MESH,
         )
-        return own, away
 
     def scatter(self, group, slot, level):
         tile = 3 * group + slot
@@ -230,21 +216,22 @@
     def places(self, index):
         expand, spatial, reduce, small = self.total
         across = expand.shape[1] // TILE
-        half = self.half_rows(self.section)
         taps = spatial.shape[0]
-        tile = index - across - taps
-        lines = pl.multiple_of(tile * TILE + self.section * self.half, 16)
+        tile, part = index // self.per_tile, index % self.per_tile
+        inside = part * self.lines + self.section * self.half
+        lines = pl.ds(pl.multiple_of(inside, 16), self.half)
+        further = pl.ds(pl.multiple_of((tile - across - taps) * TILE + inside, 16), self.half)
         return [
-            (index < across, lambda: expand.at[half, pl.ds(pl.multiple_of(index * TILE, TILE), TILE)]),
+            (tile < across, lambda: expand.at[lines, pl.ds(pl.multiple_of(tile * TILE, TILE), TILE)]),
             (
-                jnp.logical_and(index >= across, index < across + taps),
-                lambda: spatial.at[index - across, half],
+                jnp.logical_and(tile >= across, tile < across + taps),
+                lambda: spatial.at[tile - across, lines],
             ),
             (
-                jnp.logical_and(index >= across + taps, index < 2 * across + taps),
-                lambda: reduce.at[pl.ds(lines, self.half)],
+                jnp.logical_and(tile >= across + taps, tile < 2 * across + taps),
+                lambda: reduce.at[further],
             ),
-            (index == 2 * across + taps, lambda: small.at[half]),
+            (index == self.real - 1, lambda: small.at[self.half_rows(self.section)]),
         ]
 
     def final(self, tile, target):
@@ -260,9 +247,9 @@
         return here, away
 
     def finish(self, tile):
-        later = (tile >= 3 * self.groups // 2).astype(jnp.int32)
+        later = (tile >= 3 * self.block_groups).astype(jnp.int32)
         mine = self.section == 1 - later
-        index = tile - later * (3 * self.groups // 2)
+        index = tile - later * (3 * self.block_groups)
         for wanted, place in self.places(index):
 
             @pl.when(jnp.logical_and(wanted, mine))
@@ -274,7 +261,7 @@
                 self.final(tile, place())[1].start()
 
     def finished(self, tile):
-        later = (tile >= 3 * self.groups // 2).astype(jnp.int32)
+        later = (tile >= 3 * self.block_groups).astype(jnp.int32)
         mine = self.section == 1 - later
         here, away = self.final(tile, self.total[3].at[self.half_rows(self.section)])
 
@@ -287,67 +274,56 @@
 
     def stage(self, number, group):
         for slot in range(3):
-            tile = 3 * group + slot
-            if number == 0:
-                for copy in self.pair(tile):
-                    copy.start()
-            elif number == 1:
-                for copy in self.pair(tile):
-                    copy.wait()
-                self.add(self.acc(tile), [self.sec.at[tile]])
-                for copy in self.scatter(group, slot, 0):
-                    copy.start()
-            elif number in (2, 3):
-                self.scattered(group, slot, number - 2)
-                for copy in self.scatter(group, slot, number - 1):
-                    copy.start()
-            elif number == 4:
-                self.scattered(group, slot, 2)
-                for copy in self.gather(group, slot, 2):
-                    copy.start()
-            elif number in (5, 6):
-                self.gathered(group, slot, 7 - number)
-                for copy in self.gather(group, slot, 6 - number):
-                    copy.start()
-            elif number == 7:
-                self.gathered(group, slot, 0)
-                self.finish(tile)
+            if slot == 2 and self.real < 3 * self.block_groups:
+                last = lax.rem(group, self.block_groups) == self.block_groups - 1
+                pl.when(jnp.logical_not(last))(functools.partial(self.step, number, group, slot))
             else:
-                self.finished(tile)
+                self.step(number, group, slot)
+
+    def step(self, number, group, slot):
+        unit = 3 * group + slot
+        if number == 0:
+            self.pair(unit).start()
+        elif number == 1:
+            self.pair(unit).wait()
+            self.add(self.acc(unit), [self.res.at[unit]])
+            for copy in self.scatter(group, slot, 0):
+                copy.start()
+        elif number in (2, 3):
+            self.scattered(group, slot, number - 2)
+            for copy in self.scatter(group, slot, number - 1):
+                copy.start()
+        elif number == 4:
+            self.scattered(group, slot, 2)
+            for copy in self.gather(group, slot, 2):
+                copy.start()
+        elif number in (5, 6):
+            self.gathered(group, slot, 7 - number)
+            for copy in self.gather(group, slot, 6 - number):
+                copy.start()
+        elif number == 7:
+            self.gathered(group, slot, 0)
+            self.finish(unit)
+        else:
+            self.finished(unit)
 
     def tick(self, time):
+        time = jnp.asarray(time, jnp.int32)
         for number in reversed(range(self.STAGES)):
-            group = time - number
+            group = time - self.lag * number
             pl.when(jnp.logical_and(group >= 0, group < self.groups))(
                 functools.partial(self.stage, number, group)
             )
 
-
-def reduce_kernel(size, groups, parts, expand, spatial, reduce, small, *scratch):
-    reducer = Reducer(size, groups)
-    reducer.bind(parts, (expand, spatial, reduce, small), scratch)
-    reducer.greet()
-
-    @pl.loop(0, groups + reducer.STAGES - 1)
-    def _(time):
-        reducer.tick(time)
-
-
-def reduce_tiles(parts, channels, taps):
-    size = lax.axis_size("dp")
-    groups = parts.shape[0] // 3
-    reducer = Reducer(size, groups)
-    shapes = [(TILE, channels), (taps, TILE, TILE), (channels, TILE), (TILE, TILE)]
-    return pl.pallas_call(
-        functools.partial(reduce_kernel, size, groups),
-        out_shape=[jax.ShapeDtypeStruct(shape, parts.dtype) for shape in shapes],
-        in_specs=[pl.BlockSpec(memory_space=pl.ANY)],
-        out_specs=[pl.BlockSpec(memory_space=pl.ANY)] * 4,
-        scratch_shapes=reducer.scratch(),
-        compiler_params=pltpu.CompilerParams(
-            collective_id=0, has_side_effects=True, vmem_limit_bytes=LIMIT
-        ),
-    )(parts)
+    def after_tile(self, layer, tile):
+        before = (tile * self.per_tile) // 3
+        after = ((tile + 1) * self.per_tile) // 3
+        pl.when(after > before)(lambda: self.tick((1 - layer) * self.block_groups + before))
+
+    def drain(self):
+        @pl.loop(self.groups, self.groups + self.lag * (self.STAGES - 1))
+        def _(time):
+            self.tick(time)
 
 
 def silu_parts(v):
@@ -874,6 +850,7 @@
 
 def backward_kernel(
     size,
+    reducer,
     u0_hbm,
     u1_hbm,
     merged_hbm,
@@ -894,23 +871,23 @@
     hbg_ref,
     info_ref,
     grad_hbm,
-    parts,
+    expand_hbm,
+    spatial_hbm,
+    reduce_hbm,
+    small_hbm,
     wr,
     ws,
     we,
     u_ref,
     d_ref,
-    de,
     zc,
     za,
     zb,
     r1,
     r2,
-    cat,
-    dzb,
-    dza,
+    wide,
+    dz_ref,
     da,
-    stage,
     small,
     halo,
     msg,
@@ -923,9 +900,10 @@
     edge_send,
     edge_recv,
     in_sem,
-    tile_sem,
     out_sem,
+    *scratch,
 ):
+    reducer.bind((expand_hbm, spatial_hbm, reduce_hbm, small_hbm), scratch)
     link = Exchange(size, send_sem, recv_sem, edge_send, edge_recv)
     section, me = link.section, link.me
     pixels, channels = d_ref.shape
@@ -935,6 +913,7 @@
     across = channels // TILE
     f32, bf16 = jnp.float32, jnp.bfloat16
     own = pl.ds(width, pixels)
+    de, cat = wide.at[pl.ds(0, pixels)], wide.at[:, pl.ds(0, 3 * inner)]
 
     def loads(layer):
         return {
@@ -957,19 +936,18 @@
     link.greet()
     live_all = info_ref[own, 0:1]
 
-    def stage_copy(slot, tile):
-        return pltpu.make_async_copy(stage.at[slot], parts.at[tile], tile_sem.at[slot])
-
-    def put_tile(base, index, make):
-        slot = lax.rem(index, 2)
-        pl.when(base + index >= 2)(lambda: stage_copy(slot, 0).wait())
+    def put_tile(layer, tile, make):
+        unit = (1 - layer) * 3 * reducer.block_groups + tile * reducer.per_tile
 
         @pl.loop(0, 2)
         def _(side):
             cols = pl.ds(pl.multiple_of(side * 256, 256), 256)
-            stage[slot, :, cols] = make(side).astype(bf16)
-
-        stage_copy(slot, base + index).start()
+            value = make(side).astype(bf16)
+            for part in range(reducer.per_tile):
+                lines = slice(part * reducer.lines, (part + 1) * reducer.lines)
+                reducer.slot(unit + part)[:, cols] = value[lines]
+
+        reducer.after_tile(layer, tile)
 
     def column_sums(values):
         return jnp.sum(values, axis=0, keepdims=True)
@@ -980,16 +958,16 @@
             found = found + slots[step]
         return found
 
-    def expand_tiles(base):
+    def expand_tiles(layer):
         @pl.loop(0, across)
         def _(tile):
             def make(side):
                 cols = pl.ds(pl.multiple_of(tile * TILE + side * 256, 256), 256)
                 return lax.dot_general(r2[...], de[:, cols], ACROSS, preferred_element_type=f32)
 
-            put_tile(base, tile, make)
-
-    def spatial_tiles(base):
+            put_tile(layer, tile, make)
+
+    def spatial_tiles(layer):
         @pl.loop(0, 9)
         def _(tap):
             shift, side_step = tap // 3, tap % 3
@@ -999,9 +977,9 @@
                 cols = pl.ds(pl.multiple_of(side_step * inner + side * 256, 256), 256)
                 return lax.dot_general(r1[at], cat[own, cols], ACROSS, preferred_element_type=f32)
 
-            put_tile(base, across + tap, make)
-
-    def reduce_tiles_of(base, layer):
+            put_tile(layer, across + tap, make)
+
+    def reduce_tiles_of(layer):
         @pl.loop(0, across)
         def _(tile):
             def make(side):
@@ -1011,14 +989,11 @@
                     u_ref[layer, :, lines], da[:, cols], ACROSS, preferred_element_type=f32
                 )
 
-            put_tile(base, across + 9 + tile, make)
-
-    def small_tile(base, layer):
-        last = 2 * across + 9
+            put_tile(layer, across + 9 + tile, make)
+
+    def small_unit(layer):
         half = channels // 2
         head_cols = hwg_ref.shape[0]
-        slot = last % 2
-        stage_copy(slot, 0).wait()
         small[...] = jnp.zeros_like(small)
         for k in range(2):
             at = layer * half + k * TILE
@@ -1034,13 +1009,14 @@
             cols = slice(k * TILE, (k + 1) * TILE)
             small[row + 12 + k : row + 13 + k] = sums_c[1:2, cols] * only
             small[row + 12 + across + k : row + 13 + across + k] = sums_c[0:1, cols] * only
-        stage[slot] = jnp.zeros_like(stage[slot])
-        stage[slot, 0 : small.shape[0]] = small[...].astype(bf16)
-        stage_copy(slot, base + last).start()
+        unit = (1 - layer) * 3 * reducer.block_groups + reducer.real - 1
+        target = reducer.slot(unit)
+        target[...] = jnp.zeros(target.shape, bf16)
+        target[0 : small.shape[0]] = small[...].astype(bf16)
+        reducer.tick((2 - layer) * reducer.block_groups - 1)
 
     load_d.wait()
     for layer in (1, 0):
-        base = (1 - layer) * (2 * across + 10)
         now = (second, first)[layer]
         now["u"].wait()
         now["zc"].wait()
@@ -1070,8 +1046,8 @@
         for copy in sends:
             copy.start()
         if layer == 0:
-            reduce_tiles_of(0, 1)
-            small_tile(0, 1)
+            reduce_tiles_of(1)
+            small_unit(1)
         for copy in sends:
             copy.wait()
         sums_c[...] = total_of(slots)
@@ -1102,20 +1078,20 @@
             act, slope = silu_parts(normed * igs[layer, 1:2, cols] + ibs[layer, 1:2, cols])
             r2[:, cols] = act.astype(bf16)
             dz = dr2 * slope
-            dzb[:, cols] = dz
+            dz_ref[:, cols] = dz
             slots[0, 0:1, cols] = column_sums(dz)
             slots[0, 1:2, cols] = column_sums(dz * normed)
 
         sends = link.copies(3 * layer + 1, slots)
         for copy in sends:
             copy.start()
-        edges = (dzb.at[pl.ds(0, width)], dzb.at[pl.ds(pixels - width, width)])
+        edges = (dz_ref.at[pl.ds(0, width)], dz_ref.at[pl.ds(pixels - width, width)])
         landing = halo.at[layer]
         link.start_edges(layer, *edges, landing)
         if layer == 1:
             second["zc"].start()
             second["we"].start()
-        expand_tiles(base)
+        expand_tiles(layer)
         for copy in sends:
             copy.wait()
         sums[1] = total_of(slots)
@@ -1141,7 +1117,7 @@
 
         @pl.loop(0, rows)
         def _(row):
-            db_row(row + 1, dzb[pl.ds(pl.multiple_of(row * width, 16), width)], None)
+            db_row(row + 1, dz_ref[pl.ds(pl.multiple_of(row * width, 16), width)], None)
 
         if layer == 1:
             second["zb"].start()
@@ -1161,7 +1137,7 @@
             normed = za[:, cols].astype(f32)
             _, slope = silu_parts(normed * igs[layer, 0:1, cols] + ibs[layer, 0:1, cols])
             dz = dr1 * slope
-            dza[:, cols] = dz
+            dz_ref[:, cols] = dz
             slots[0, 0:1, cols] = column_sums(dz)
             slots[0, 1:2, cols] = column_sums(dz * normed)
 
@@ -1171,7 +1147,7 @@
         if layer == 1:
             second["ws"].start()
         now["r1"].wait()
-        spatial_tiles(base)
+        spatial_tiles(layer)
         for copy in sends:
             copy.wait()
         sums[0] = total_of(slots)
@@ -1183,7 +1159,7 @@
             here = pl.ds(pl.multiple_of(row * width, 16), width)
             live = info_ref[pl.ds(pl.multiple_of((row + 1) * width, 16), width), 0:1]
             away = (sums[0, 0:1] + za[here].astype(f32) * sums[0, 1:2]) * share
-            value = (rs_ref[layer, 0:1] * igs[layer, 0:1]) * (dza[here] - live * away)
+            value = (rs_ref[layer, 0:1] * igs[layer, 0:1]) * (dz_ref[here] - live * away)
             da[here] = value.astype(bf16)
 
         if layer == 1:
@@ -1200,10 +1176,9 @@
             second["wr"].start()
     out = pltpu.make_async_copy(d_ref, grad_hbm, out_sem)
     out.start()
-    reduce_tiles_of(2 * across + 10, 0)
-    small_tile(2 * across + 10, 0)
-    stage_copy(0, 0).wait()
-    stage_copy(1, 0).wait()
+    reduce_tiles_of(0)
+    small_unit(0)
+    reducer.drain()
     out.wait()
 
 
@@ -1216,15 +1191,17 @@
     f32, bf16 = jnp.float32, jnp.bfloat16
     anywhere = pl.BlockSpec(memory_space=pl.ANY)
     vmem = pl.BlockSpec(memory_space=pltpu.VMEM)
-    count = 2 * (2 * (channels // TILE) + 10)
+    taps = ws.shape[1]
+    reducer = Reducer(size, 2 * (channels // TILE) + taps)
+    totals = [(TILE, channels), (taps, TILE, TILE), (channels, TILE), (reducer.lines, TILE)]
     return pl.pallas_call(
-        functools.partial(backward_kernel, size),
+        functools.partial(backward_kernel, size, reducer),
         out_shape=[
             jax.ShapeDtypeStruct((pixels, channels), bf16),
-            jax.ShapeDtypeStruct((count, TILE, TILE), bf16),
-        ],
+        ]
+        + [jax.ShapeDtypeStruct(shape, bf16) for shape in totals],
         in_specs=[anywhere] * 10 + [vmem] * 9,
-        out_specs=[anywhere] * 2,
+        out_specs=[anywhere] * 5,
         scratch_shapes=[
             pltpu.VMEM((channels, inner), bf16),
             pltpu.VMEM((9, inner, inner), bf16),
@@ -1232,16 +1209,13 @@
             pltpu.VMEM((2, pixels, channels), bf16),
             pltpu.VMEM((pixels, channels), bf16),
             pltpu.VMEM((pixels, channels), bf16),
-            pltpu.VMEM((pixels, channels), bf16),
             pltpu.VMEM((pixels, inner), bf16),
             pltpu.VMEM((padded, inner), bf16),
             pltpu.VMEM((padded, inner), bf16),
             pltpu.VMEM((pixels, inner), bf16),
-            pltpu.VMEM((padded, 3 * inner), bf16),
-            pltpu.VMEM((pixels, inner), f32),
+            pltpu.VMEM((padded, channels), bf16),
             pltpu.VMEM((pixels, inner), f32),
             pltpu.VMEM((pixels, inner), bf16),
-            pltpu.VMEM((2, TILE, TILE), bf16),
             pltpu.VMEM((128, TILE), f32),
             pltpu.VMEM((2, 2, width, inner), f32),
             pltpu.VMEM((4, size, 2, inner), f32),
@@ -1254,11 +1228,11 @@
             pltpu.SemaphoreType.DMA((2, 2)),
             pltpu.SemaphoreType.DMA((2, 2)),
             pltpu.SemaphoreType.DMA((10,)),
-            pltpu.SemaphoreType.DMA((2,)),
             pltpu.SemaphoreType.DMA,
-        ],
+        ]
+        + reducer.scratch(),
         compiler_params=pltpu.CompilerParams(
-            collective_id=2, has_side_effects=True, vmem_limit_bytes=LIMIT
+            collective_id=2, has_side_effects=True, vmem_limit_bytes=63 * 2**20
         ),
     )(u0, u1, merged, zc, za, zb, r1, wr, ws, we, igs, ibs, ogs, obs, rs, rc, hwg, hbg, info)
 
@@ -1306,7 +1280,6 @@
     section = lax.axis_index("section")
     first = section == 0
     rows, width, channels = canvases.shape[1:]
-    taps = spatial_weight.shape[1]
     head_cols = head_weight.shape[1]
     pixels = rows * width
     flat = canvases.reshape(pixels, channels)
@@ -1326,10 +1299,9 @@
         head_bias[None],
         info,
     )
-    grad, parts = backward(
+    grad, expand_total, spatial_total, reduce_total, small = backward(
         flat, u1, merged, zc, za, zb, r1, wr, ws, we, igs, ibs, ogs, obs, rs, rc, hwg, hbg, info
     )
-    expand_total, spatial_total, reduce_total, small = reduce_tiles(parts, channels, taps)
     small = small.astype(jnp.float32)
     half = channels // 2
     across = channels // TILE

time: 397 us -> 350 us (0.88)
  Pallas kernels: 360 us -> 318 us
    pallas_call x2 -> x1, Pallas kernels: 267 us -> 224 us  [backward(): pl.pallas_call(functools.partial(backward_kernel, size, reducer), out_sha...]
where the time goes in v3:
time: 350 us
  Pallas kernels  318 us (91%)
  other arithmetic  15.6 us (4%)
  local copies, waits for them, and re-layouts  8.44 us (2%)
  starting transfers between devices  6.12 us (2%)
    pallas_call x1, Pallas kernels, backward(): pl.pallas_call(functools.partial(backward_kernel, size, reducer), out_sha...  224 us
    pallas_call x1, Pallas kernels, forward(): pl.pallas_call(functools.partial(forward_kernel, size), out_shape=[out(f3...  93.6 us
  transfers between devices with their start and end apart: 2, of which 1 were waited for; matrix products, arithmetic and copies ran while one was open for 1% of the time, Pallas kernels for 0%

profile of v3, /device:TPU:0, one launch (start us, length us, event | category | flops | bytes accessed | tf_op | source)
XLA Modules:
  0.0 349.7 jit_solution(15590161640906464174)
XLA Ops:
  0.7 0.7 copy-done
  1.4 4.8 %collective-permute-start = (s32[1,96]{1,0:T(1,128)S(1)}, s32[1,96]{1,0:T(1,128)S(1)}, u32[]{:S(2)}, u32[]{:S(2)}) collective-permute-start(s32[1,96]{1,0:T(1,128)S(1)} %get-tuple-element.85), channel_id=1, source_target_pairs={{0,1},{1,2},{2,3},{3,4},{4,5},{5,6},{6,7},{7,8},{8,9},{9,10},{10,1... | collective-permute-start | bytes 1160 | tf_op jit(solution)/shard_map/ppermute | solution.py:1245
  6.2 1.3 collective-permute-start.1
  7.5 0.7 dynamic-slice_bitcast_fusion
  8.2 0.1 convert_reduce_fusion
  8.4 0.1 compare_convert_fusion.1
  8.5 0.1 select_add_fusion
  8.6 1.9 copy.27.cot_hbm
  10.4 1.2 collective-permute-done.1
  11.7 1.0 fusion.info_ref
  12.7 93.6 %shard_map.221 = (f32[768,48]{1,0:T(8,128)}, f32[48,2048]{1,0:T(8,128)}, f32[1,48]{1,0:T(1,128)}, f32[2,2,512]{2,1,0:T(2,128)}, f32[2,2,512]{2,1,0:T(2,128)}, /*...) custom-call(bf16[768,2048]{1,0:T(8,128)(2,1)} %bitcast.49, ...), custom_call_target="tpu_custom_call" | custom-call | tf_op jit(solution)/shard_map/pallas_call | solution.py:786
  106.3 224.0 %shard_map.222 = (bf16[768,2048]{1,0:T(8,128)(2,1)}, bf16[512,2048]{1,0:T(8,128)(2,1)}, bf16[9,512,512]{2,1,0:T(8,128)(2,1)}, bf16[2048,512]{1,0:T(8,128)(2,1)}, bf16[256,512]{1,0:T(8,128)(2,1)}) custom-call(bf16[768,2048]{1,0:T(8,128)(2,1)} %bitcast.50, bf16[768,2048]{1,0:T(8,128)(2,1)} %get-tuple-element.35.u1_hbm, ...), custom_call_target="tpu_custom_call" | custom-call | tf_op jit(solution)/shard_map/pallas_call | solution.py:1197
  330.3 1.1 convert_element_type.33
  331.4 0.6 slice_bitcast_fusion.4
  332.0 0.7 slice_bitcast_fusion.1
  332.7 0.8 copy.28
  333.6 0.6 fusion.1
  334.1 0.6 copy.30
  334.8 0.6 copy.29
  335.4 4.3 %bitcast_convert_fusion.2 = f32[1,2048,512]{2,1,0:T(8,128)} fusion(bf16[2048,512]{1,0:T(8,128)(2,1)} %get-tuple-element.53), kind=kLoop, calls=%fused_computation.2 | loop fusion | flops 1048576 | bytes 6291456 | tf_op jit(solution)/shard_map/broadcast_in_dim | solution.py:1316
  339.7 2.5 bitcast_convert_fusion.1
  342.3 5.1 %bitcast_convert_fusion = f32[1,9,512,512]{3,2,1,0:T(8,128)} fusion(bf16[9,512,512]{2,1,0:T(8,128)(2,1)S(1)} %bitcast.52), kind=kLoop, calls=%fused_computation | loop fusion | flops 2359296 | bytes 14155776 | tf_op jit(solution)/shard_map/broadcast_in_dim | solution.py:1317
  347.4 0.7 pad_maximum_fusion
  348.1 1.7 copy.32
  (28 shorter events, 0.2 us)
Async XLA Ops:
  0.6 0.7 copy-start
  1.4 9.1 %collective-permute-start = (s32[1,96]{1,0:T(1,128)S(1)}, s32[1,96]{1,0:T(1,128)S(1)}, u32[]{:S(2)}, u32[]{:S(2)}) collective-permute-start(s32[1,96]{1,0:T(1,128)S(1)} %get-tuple-element.85), channel_id=1, source_target_pairs={{0,1},{1,2},{2,3},{3,4},{4,5},{5,6},{6,7},{7,8},{8,9},{9,10},{10,1... | collective-permute-start | bytes 1160 | tf_op jit(solution)/shard_map/ppermute | solution.py:1245
  6.2 5.4 %collective-permute-start.1 = (s32[1,96]{1,0:T(1,128)S(1)}, s32[1,96]{1,0:T(1,128)S(1)}, u32[]{:S(2)}, u32[]{:S(2)}) collective-permute-start(s32[1,96]{1,0:T(1,128)S(1)} %get-tuple-element.86), channel_id=1, source_target_pairs={{1,0},{2,1},{3,2},{4,3},{5,4},{6,5},{7,6},{8,7},{9,8},{10,9},{11,1... | collective-permute-start | bytes 1160 | tf_op jit(solution)/shard_map/ppermute | solution.py:1246
  106.3 226.5 %copy-start.4 = (f32[768,48]{1,0:T(8,128)S(1)}, f32[768,48]{1,0:T(8,128)}, u32[]{:S(2)}) copy-start(f32[768,48]{1,0:T(8,128)} %get-tuple-element.34) | copy-start | bytes 442372
  330.3 9.5 %copy-start.3 = (bf16[512,2048]{1,0:T(8,128)(2,1)S(1)}, bf16[512,2048]{1,0:T(8,128)(2,1)}, u32[]{:S(2)}) copy-start(bf16[512,2048]{1,0:T(8,128)(2,1)} %get-tuple-element.55) | copy-start | bytes 6291460
  332.7 9.5 %slice-start = ((s8[4718592]{0:T(1024)(128)(4,1)}), s8[524288]{0:T(1024)(128)(4,1)S(1)}, s32[]{:S(2)}) async-start(s8[4718592]{0:T(1024)(128)(4,1)} %bitcast.51), calls=%async_computation | async-start | bytes 1048576
  335.4 6.9 %slice-start.1 = ((s8[4718592]{0:T(1024)(128)(4,1)}), s8[4194304]{0:T(1024)(128)(4,1)S(1)}, s32[]{:S(2)}) async-start(s8[4718592]{0:T(1024)(128)(4,1)} %bitcast.51), calls=%async_computation.1 | async-start | bytes 8388608
  342.3 5.1 %copy-start.5 = (f32[512,48]{0,1:T(8,128)S(1)}, f32[512,48]{0,1:T(8,128)}, u32[]{:S(2)}) copy-start(f32[512,48]{0,1:T(8,128)} %get-tuple-element.79) | copy-start | bytes 294916
  342.3 5.1 %copy-start.6 = (f32[512,48]{0,1:T(8,128)S(1)}, f32[512,48]{0,1:T(8,128)}, u32[]{:S(2)}) copy-start(f32[512,48]{0,1:T(8,128)} %get-tuple-element.80) | copy-start | bytes 294916
  342.3 5.8 %copy-start.2 = (bf16[768,2048]{1,0:T(8,128)(2,1)S(1)}, bf16[768,2048]{1,0:T(8,128)(2,1)}, u32[]{:S(2)}) copy-start(bf16[768,2048]{1,0:T(8,128)(2,1)} %get-tuple-element.52) | copy-start | bytes 9437188
  342.3 7.4 %copy-start.1 = (s32[2,8,96]{2,1,0:T(8,128)S(1)}, s32[2,8,96]{2,1,0:T(8,128)}, u32[]{:S(2)}) copy-start(s32[2,8,96]{2,1,0:T(8,128)} %param.16) | copy-start | bytes 18436
